TPU v7x, 256 devices: a whole 4x4x8 slice. The times are simulated.
256 devices in a mesh: ctx: 64 (over x, z, core), section: 4 (over y).
Axes of the slice: x: 4, y: 4, z: 8, core: 2. Of those that a mesh axis runs over, the one named last changes fastest.
Arguments:
- query_heads: bfloat16 [4, 8192, 4096], P('section', 'ctx'), may hold values from -12 to 12
- key_heads: bfloat16 [4, 8192, 512], P('section', 'ctx'), may hold values from -12 to 12
- value_heads: bfloat16 [4, 8192, 512], P('section', 'ctx'), may hold values from -6 to 6
- attn_output: bfloat16 [4, 8192, 4096], P('section', 'ctx'), may hold values from -6 to 6
- output_grad: bfloat16 [4, 8192, 4096], P('section', 'ctx'), may hold values from -6 to 6
- doc_start: int32 [8192], P('ctx'), may hold values from 0 to 8191, as said below
- fetch_list: int32 [64, 2], P('ctx'), may hold values from 0 to 1, as said below
Outputs:
- handed_grad: bfloat16 [4, 8192, 4096], P('section', 'ctx')
- key_grad: bfloat16 [4, 8192, 512], P('section', 'ctx')
- value_grad: bfloat16 [4, 8192, 512], P('section', 'ctx')
Inputs may be any that keep to these rules, and one draw needn't show every extreme that they name: doc_start never falls, doc_start[t] <= t, and positions with equal doc_start form one document; a document holds at most 257 positions, and some hold exactly that many; the last position forms a document of its own. fetch_list[i, d - 1] is 1 exactly when some position of shard i and some position of shard i - d lie in one document.
All inputs are finite; a program needn't handle non-finite values.
Results may differ from a plain program's by a relative error of at most 0.0095.
Values may be sent and summed in bfloat16 or wider, within the bound.
A program may use at most 64 MiB of HBM per device.

v0:
```python
import math

import jax
import jax.numpy as jnp
from jax import lax
from jax.sharding import PartitionSpec as P

HQ = 32
HK = 4
HD = 128
FETCH = 2


ROPE_BASE = 1000000.0
TRAINED_CONTEXT = 32768.0
YARN_FACTOR = 4.0
NEG_LARGE = -1e30


def from_behind(value, axis, steps):
    count = lax.axis_size(axis)
    initial, last = (max(0, -steps), min(count, count - steps))
    return lax.ppermute(value, axis, [(source, source + steps) for source in range(initial, last)])


def yarn_frequencies(head_dim):
    half_dim = head_dim // 2

    def correction(rotations):
        return (
            head_dim
            * math.log(TRAINED_CONTEXT / (rotations * 2.0 * math.pi))
            / (2.0 * math.log(ROPE_BASE))
        )

    lower_dim = max(math.floor(correction(32.0)), 0)
    upper_dim = min(math.ceil(correction(1.0)), head_dim - 1)
    spread_dims = max(upper_dim - lower_dim, 0.001)
    indices = jnp.arange(half_dim, dtype=jnp.float32)
    extrapolated = jnp.power(jnp.float32(ROPE_BASE), -2.0 * indices / head_dim)
    ramp_weight = jnp.clip((indices - lower_dim) / spread_dims, 0.0, 1.0)
    return extrapolated / YARN_FACTOR * ramp_weight + extrapolated * (1.0 - ramp_weight)


def rope_tables(positions, head_dim):
    freqs = yarn_frequencies(head_dim)
    angles = positions.astype(jnp.float32)[:, None] * freqs[None, :]
    angles = jnp.concatenate([angles, angles], axis=1)
    factor = 0.1 * math.log(YARN_FACTOR) + 1.0
    return ((jnp.cos(angles) * factor)[:, None, :], (jnp.sin(angles) * factor)[:, None, :])


def apply_rope(inputs, cosine, sine_table):
    half_dim = inputs.shape[-1] // 2
    turned = jnp.concatenate([-inputs[..., half_dim:], inputs[..., :half_dim]], axis=-1)
    return inputs * cosine + turned * sine_table


def undo_rope(grads, cosine, sine_table):
    half_dim = grads.shape[-1] // 2
    scaled = grads * sine_table
    return grads * cosine + jnp.concatenate(
        [scaled[..., half_dim:], -scaled[..., :half_dim]], axis=-1
    )


def shards(query_heads, key_heads, value_heads, attn_output, output_grad, doc_start, fetch_list):
    tok_rows = query_heads.shape[1]
    ratio = HQ // HK
    score_scale = HD ** (-0.5)
    first_row = lax.axis_index("ctx") * tok_rows
    block_idx = jnp.arange(tok_rows, dtype=jnp.int32)
    t_pos = first_row + block_idx
    cosine, sine_table = rope_tables(t_pos - doc_start, HD)
    q_rot = apply_rope(
        query_heads[0].astype(jnp.float32).reshape(tok_rows, HQ, HD), cosine, sine_table
    )
    q_rot = q_rot.astype(jnp.bfloat16).reshape(tok_rows, HK, ratio, HD)
    k_rot = apply_rope(
        key_heads[0].astype(jnp.float32).reshape(tok_rows, HK, HD), cosine, sine_table
    ).astype(jnp.bfloat16)
    val_rows = value_heads[0].reshape(tok_rows, HK, HD)
    grad_rows = output_grad[0].reshape(tok_rows, HK, ratio, HD)
    delta = jnp.sum(
        (output_grad[0].astype(jnp.float32) * attn_output[0].astype(jnp.float32)).reshape(
            tok_rows, HK, ratio, HD
        ),
        axis=-1,
    )
    listed = fetch_list[0]
    blocks = [(k_rot, val_rows)]
    for distance in range(1, FETCH + 1):
        blocks.append(from_behind((k_rot, val_rows), "ctx", distance))
    masks = []
    for distance in range(FETCH + 1):
        u_pos = first_row - distance * tok_rows + block_idx
        masks.append((u_pos[None, :] >= doc_start[:, None]) & (u_pos[None, :] <= t_pos[:, None]))
    stat_shape = (tok_rows, HK, ratio)
    empty_stats = (jnp.full(stat_shape, NEG_LARGE, jnp.float32), jnp.zeros(stat_shape, jnp.float32))

    def tile_stats(k_blk, allowed):
        scores = (
            jnp.einsum("tgre,uge->tgru", q_rot, k_blk, preferred_element_type=jnp.float32)
            * score_scale
        )
        pair_mask = allowed[:, None, None, :]
        largest = jnp.max(jnp.where(pair_mask, scores, NEG_LARGE), axis=-1)
        exp_total = jnp.sum(
            jnp.where(pair_mask, jnp.exp(scores - largest[..., None]), 0.0), axis=-1
        )
        return (largest, exp_total)

    all_stats = [tile_stats(blocks[0][0], masks[0])]
    for distance in range(1, FETCH + 1):
        all_stats.append(
            lax.cond(
                listed[distance - 1] == 1,
                lambda k_blk=blocks[distance][0], allowed=masks[distance]: tile_stats(
                    k_blk, allowed
                ),
                lambda: empty_stats,
            )
        )
    overall = all_stats[0][0]
    for stats in all_stats[1:]:
        overall = jnp.maximum(overall, stats[0])
    summed = jnp.zeros(stat_shape, jnp.float32)
    for stats in all_stats:
        summed = summed + stats[1] * jnp.exp(stats[0] - overall)
    lse = overall + jnp.log(summed)

    def tile_grads(k_blk, v_blk, allowed):
        scores = (
            jnp.einsum("tgre,uge->tgru", q_rot, k_blk, preferred_element_type=jnp.float32)
            * score_scale
        )
        pair_mask = allowed[:, None, None, :]
        prob = jnp.where(pair_mask, jnp.exp(scores - lse[..., None]), 0.0)
        prob_b = prob.astype(jnp.bfloat16)
        dprob = jnp.einsum("tgre,uge->tgru", grad_rows, v_blk, preferred_element_type=jnp.float32)
        dscore = (prob * (dprob - delta[..., None])).astype(jnp.bfloat16)
        dq_part = (
            jnp.einsum("tgru,uge->tgre", dscore, k_blk, preferred_element_type=jnp.float32)
            * score_scale
        )
        dk_part = (
            jnp.einsum("tgru,tgre->uge", dscore, q_rot, preferred_element_type=jnp.float32)
            * score_scale
        )
        dv_part = jnp.einsum(
            "tgru,tgre->uge", prob_b, grad_rows, preferred_element_type=jnp.float32
        )
        return (dq_part, dk_part, dv_part)

    zero_kv = jnp.zeros((tok_rows, HK, HD), jnp.float32)
    empty_grads = (jnp.zeros((tok_rows, HK, ratio, HD), jnp.float32), zero_kv, zero_kv)
    own_grads = tile_grads(blocks[0][0], blocks[0][1], masks[0])
    dq_sum = own_grads[0]
    contributions = [(own_grads[1], own_grads[2])]
    for distance in range(1, FETCH + 1):
        tile_result = lax.cond(
            listed[distance - 1] == 1,
            lambda k_blk=blocks[distance][0], v_blk=blocks[distance][1], allowed=masks[
                distance
            ]: tile_grads(k_blk, v_blk, allowed),
            lambda: empty_grads,
        )
        dq_sum = dq_sum + tile_result[0]
        contributions.append((tile_result[1], tile_result[2]))
    returned = (zero_kv, zero_kv)
    for distance in range(1, FETCH + 1):
        arrived = from_behind(contributions[distance], "ctx", -distance)
        returned = (returned[0] + arrived[0], returned[1] + arrived[1])
    dk_total = contributions[0][0] + returned[0]
    dv_total = contributions[0][1] + returned[1]
    key_grad = (
        undo_rope(dk_total, cosine, sine_table).astype(jnp.bfloat16).reshape(1, tok_rows, HK * HD)
    )
    value_grad = dv_total.astype(jnp.bfloat16).reshape(1, tok_rows, HK * HD)
    query_grad = (
        undo_rope(dq_sum.reshape(tok_rows, HQ, HD), cosine, sine_table)
        .astype(jnp.bfloat16)
        .reshape(1, tok_rows, HQ * HD)
    )
    handed_grad = from_behind(query_grad, "section", -1)
    return (handed_grad, key_grad, value_grad)


def solution(mesh):
    return jax.shard_map(
        shards,
        mesh=mesh,
        in_specs=(
            P("section", "ctx", None),
            P("section", "ctx", None),
            P("section", "ctx", None),
            P("section", "ctx", None),
            P("section", "ctx", None),
            P("ctx"),
            P("ctx", None),
        ),
        out_specs=(P("section", "ctx", None), P("section", "ctx", None), P("section", "ctx", None)),
        check_vma=False,
    )
```

profile of v0, /device:TPU:20, one launch (start us, length us, event | category | flops | bytes accessed | tf_op | source)
XLA Modules:
  0.0 119.7 jit_solution(7406971572263412723)
XLA Ops:
  0.7 1.1 copy.81
  1.8 0.7 subtract_convert_fusion
  2.8 0.7 fusion.53
  3.5 3.8 %collective-permute-start.1 = (bf16[128,4,128]{0,2,1:T(8,128)(2,1)}, bf16[128,4,128]{0,2,1:T(8,128)(2,1)S(1)}, u32[]{:S(2)}, u32[]{:S(2)}) collective-permute-start(bf16[128,4,128]{0,2,1:T(8,128)(2,1)} %fusion.53), channel_id=1, source_target_pairs={{0,8},{4,12},{8,16},{12,20},{16,24},{20,28},{24,32},{28,36},{32,40... | collective-permute-start | bytes 393224 | tf_op jit(solution)/shard_map/ppermute | solution.py:23
  7.3 1.9 %collective-permute-start = (bf16[128,4,128]{0,2,1:T(8,128)(2,1)}, bf16[128,4,128]{0,2,1:T(8,128)(2,1)S(1)}, u32[]{:S(2)}, u32[]{:S(2)}) collective-permute-start(bf16[128,4,128]{0,2,1:T(8,128)(2,1)} %fusion.53), channel_id=1, source_target_pairs={{0,4},{4,8},{8,12},{12,16},{16,20},{20,24},{24,28},{28,32},{32,36}... | collective-permute-start | bytes 393224 | tf_op jit(solution)/shard_map/ppermute | solution.py:23
  9.2 1.7 %copy.89 = bf16[1,128,512]{1,2,0:T(8,128)(2,1)} copy(bf16[1,128,512]{2,1,0:T(8,128)(2,1)} %param.17) | data formatting | bytes 262144 | tf_op args[2]
  10.9 3.8 %collective-permute-start.3 = (bf16[128,4,128]{0,2,1:T(8,128)(2,1)}, bf16[128,4,128]{0,2,1:T(8,128)(2,1)}, u32[]{:S(2)}, u32[]{:S(2)}) collective-permute-start(bf16[128,4,128]{0,2,1:T(8,128)(2,1)} %bitcast.37), channel_id=1, source_target_pairs={{0,8},{4,12},{8,16},{12,20},{16,24},{20,28},{24,32},{28,36},{32,40... | collective-permute-start | bytes 393224 | tf_op jit(solution)/shard_map/ppermute | solution.py:23
  14.7 3.7 %collective-permute-start.2 = (bf16[128,4,128]{0,2,1:T(8,128)(2,1)}, bf16[128,4,128]{0,2,1:T(8,128)(2,1)}, u32[]{:S(2)}, u32[]{:S(2)}) collective-permute-start(bf16[128,4,128]{0,2,1:T(8,128)(2,1)} %bitcast.37), channel_id=1, source_target_pairs={{0,4},{4,8},{8,12},{12,16},{16,20},{20,24},{24,28},{28,32},{32,36}... | collective-permute-start | bytes 393224 | tf_op jit(solution)/shard_map/ppermute | solution.py:23
  18.4 0.7 copy.105
  19.1 0.6 fusion.72
  20.4 0.7 copy.82
  21.2 1.5 %slice_negate_fusion.1 = (f32[128,32,64]{0,2,1:T(8,128)}, f32[128,32,64]{0,2,1:T(8,128)}) fusion(f32[128,32,128]{0,2,1:T(8,128)S(1)} %bitcast.224), kind=kLoop, calls=%fused_computation.74 | loop fusion | flops 262144 | bytes 4194304 | tf_op jit(solution)/shard_map/neg | solution.py:55
  22.7 0.5 copy-done.1
  23.9 0.7 copy.90
  24.6 1.3 %copy.93 = bf16[1,128,4096]{1,2,0:T(8,128)(2,1)} copy(bf16[1,128,4096]{2,1,0:T(8,128)(2,1)S(1)} %copy-done.6) | data formatting | bytes 2097152 | tf_op args[3]
  25.9 1.0 mul.241
  26.9 1.5 %mul.242 = f32[1,128,4096]{2,1,0:T(8,128)} reshape(f32[128,32,128]{2,1,0:T(8,128)S(1)} %mul.241) | data formatting | bytes 4194304 | tf_op jit(solution)/shard_map/mul | solution.py:56
  28.6 2.7 %fusion.33 = bf16[128,4,8,128]{0,3,2,1:T(8,128)(2,1)S(1)} fusion(f32[128,4,8,64]{0,3,2,1:T(8,128)} %bitcast.230, f32[128,4,8,64]{0,3,2,1:T(8,128)} %bitcast.229, f32[128,4,8,128]{0,3,2,1:T(8,128)} %bitcast.225, f32[128,128]{0,1:T(8,128)S(1)} %get-tuple-element.167, f32[128,128]{0,1:T(8,128)S(1)} %get-tuple-element.166), kind=kLoop, calls=%fused_computation.48 | loop fusion | flops 2621440 | bytes 5373952 | tf_op jit(solution)/shard_map/convert_element_type | solution.py:78
  31.3 1.5 %fusion.38 = (f32[128,4,8]{0,2,1:T(8,128)S(1)}, f32[4,128,128,8]{2,1,3,0:T(8,128)S(1)}) fusion(pred[128,128]{0,1:T(8,128)(4,1)S(1)} %get-tuple-element.168, bf16[128,4,8,128]{0,3,2,1:T(8,128)(2,1)S(1)} %fusion.33, bf16[128,4,128]{0,2,1:T(8,128)(2,1)} %fusion.53), kind=kOutput, calls=%fused_computation.61 | convolution fusion | flops 135786496 | bytes 3309568 | tf_op jit(solution)/shard_map/tgre,uge->tgru/dot_general | solution.py:134
  32.8 0.5 fusion.41
  33.3 0.4 fusion.34
  33.7 0.4 copy-done
  34.1 0.6 conditional.5
  34.1 0.6 broadcast_in_dim.105
  34.8 2.3 %conditional.4 = (f32[128,4,8]{0,2,1:T(8,128)}, f32[128,4,8]{0,2,1:T(8,128)S(1)}) conditional(s32[]{:T(128)} %bitcast.35, () %tuple.40, (pred[128,128]{0,1:T(8,128)(4,1)S(1)}, bf16[128,4,128]{0,2,1:T(8,128)(2,1)S(1)}, bf16[128,4,8,128]{0,3,2,1:T(8,128)(2,1)S(1)}) %tuple.41), branch_computations={%region_1.2_spmd, %region_2.0_spmd} | conditional | flops 137879552 | bytes 5455888 | solution.py:116
  34.8 1.1 fusion
  35.9 1.2 fusion.3
  37.1 0.8 log_add_fusion
  37.9 2.3 %fusion.37 = bf16[128,4,8,128]{0,3,2,1:T(8,128)(2,1)S(1)} fusion(bf16[128,4,128,1]{0,2,3,1:T(8,128)(2,1)} %bitcast.71, bf16[128,4,8,128]{0,3,2,1:T(8,128)(2,1)S(1)} %bitcast.220, f32[4,128,128,8]{2,1,3,0:T(8,128)} %copy-done, f32[128,4,8]{0,2,1:T(8,128)S(1)} %fusion.34, f32[128,4,8]{0,2,1:T(8,128)S(1)} %log_add_fusion, pred[128,128]{0,1:T(8,128)(4,1)} %copy-done.7), kind=kOutput, calls=%fused_computation.57 | convolution fusion | flops 137363456 | bytes 4374528 | tf_op jit(solution)/shard_map/tgre,uge->tgru/dot_general | solution.py:140
  40.2 2.7 %fusion.57 = f32[4,128,128,8]{2,1,3,0:T(8,128)} fusion(bf16[128,4,8,128]{0,3,2,1:T(8,128)(2,1)S(1)} %fusion.37, bf16[128,4,128]{0,2,1:T(8,128)(2,1)} %fusion.53), kind=kOutput, calls=%fused_computation.90 | convolution fusion | flops 134217728 | bytes 3276800 | tf_op jit(solution)/shard_map/tgru,uge->tgre/dot_general | solution.py:143
  42.9 3.1 %conditional.7 = (f32[128,4,128]{2,0,1:T(8,128)}, f32[128,4,128]{2,0,1:T(8,128)}, f32[128,4,8,128]{0,3,2,1:T(8,128)}) conditional(s32[]{:T(128)} %bitcast.36, () %tuple.46, (pred[128,128]{0,1:T(8,128)(4,1)S(1)}, bf16[128,4,128]{0,2,1:T(8,128)(2,1)S(1)}, bf16[128,4,8,128]{0,3,2,1:T(8,128)(2,1)S(1)}, f32[128,4,8]{0,2,1:T(8,128)S(1)}, ...), branch_computations={%region_13.14_spmd, %region_14.15_spmd} | conditional | flops 675348480 | bytes 20889624 | solution.py:161
  42.9 0.7 broadcast_in_dim.115
  43.6 0.7 broadcast_in_dim.115.clone
  44.4 1.6 %broadcast_in_dim.114.clone = f32[128,4,8,128]{0,3,2,1:T(8,128)} broadcast(f32[]{:T(128)} %constant.48.clone), dimensions={} | broadcast | bytes 2097156 | tf_op jit(solution)/shard_map/broadcast_in_dim | solution.py:156
  46.0 10.0 %conditional.6 = (f32[128,4,128]{2,0,1:T(8,128)}, f32[128,4,128]{2,0,1:T(8,128)}, f32[128,4,8,128]{0,3,2,1:T(8,128)}) conditional(s32[]{:T(128)} %bitcast.35, () %tuple.44, (pred[128,128]{0,1:T(8,128)(4,1)}, bf16[128,4,128]{0,2,1:T(8,128)(2,1)S(1)}, bf16[128,4,8,128]{0,3,2,1:T(8,128)(2,1)S(1)}, f32[128,4,8]{0,2,1:T(8,128)}, ...), branch_computations={%region_11.12_spmd, %region_12.13_spmd} | conditional | flops 675348480 | bytes 20889624 | solution.py:161
  46.0 1.3 %fusion.15 = f32[128,4,8,128]{0,3,2,1:T(8,128)S(1)} fusion(bf16[128,4,8,128]{0,3,2,1:T(8,128)(2,1)S(1)} %get-tuple-element.137, f32[128,4,8]{0,2,1:T(8,128)} %get-tuple-element.49, pred[128,128]{0,1:T(8,128)(4,1)} %get-tuple-element.46, bf16[128,4,128]{0,2,1:T(8,128)(2,1)S(1)} %get-tuple-element.136), kind=kOutput, calls=%fused_computation.21 | convolution fusion | flops 135790592 | bytes 3309568 | tf_op jit(solution)/shard_map/cond/branch_1_fun/tgre,uge->tgru/dot_general | solution.py:134
  47.3 1.4 %fusion.13 = bf16[128,4,8,128]{0,3,2,1:T(8,128)(2,1)S(1)} fusion(f32[128,4,8,128]{0,3,2,1:T(8,128)S(1)} %fusion.15, bf16[128,4,8,128]{0,3,2,1:T(8,128)(2,1)S(1)} %get-tuple-element.140, f32[128,4,8]{0,2,1:T(8,128)S(1)} %get-tuple-element.52, bf16[128,4,128]{0,2,1:T(8,128)(2,1)} %get-tuple-element.139), kind=kOutput, calls=%fused_computation.18 | convolution fusion | flops 135790592 | bytes 4341760 | tf_op jit(solution)/shard_map/cond/branch_1_fun/tgre,uge->tgru/dot_general | solution.py:140
  48.8 1.2 fusion.17
  49.9 1.2 convolution_bitcast_fusion
  51.1 1.9 %multiply_bitcast_fusion = f32[128,4,8,128]{3,0,2,1:T(8,128)} fusion(bf16[128,4,8,128]{0,3,2,1:T(8,128)(2,1)S(1)} %fusion.13, bf16[128,4,128]{0,2,1:T(8,128)(2,1)S(1)} %get-tuple-element.136), kind=kOutput, calls=%fused_computation.22 | convolution fusion | flops 134742016 | bytes 3276800 | tf_op jit(solution)/shard_map/cond/branch_1_fun/tgru,uge->tgre/dot_general | solution.py:143
  53.0 3.0 %copy.162 = f32[128,4,8,128]{0,3,2,1:T(8,128)} copy(f32[128,4,8,128]{3,0,2,1:T(8,128)} %multiply_bitcast_fusion) | data formatting | bytes 4194304 | tf_op jit(solution)/shard_map/cond | solution.py:161
  56.0 3.4 %fusion.35 = f32[128,4,8,128]{0,3,2,1:T(8,128)S(1)} fusion(f32[128,4,8,128]{0,3,2,1:T(8,128)} %get-tuple-element.153, f32[128,4,8,128]{0,3,2,1:T(8,128)} %get-tuple-element.152, f32[4,128,128,8]{2,1,3,0:T(8,128)} %fusion.57), kind=kLoop, calls=%fused_computation.54 | loop fusion | flops 1572864 | bytes 8388608 | tf_op jit(solution)/shard_map/add | solution.py:168
  59.6 1.1 copy-done.2
  61.0 1.5 %pad_maximum_fusion = f32[128,32,128]{0,2,1:T(8,128)} fusion(f32[128,32,64]{0,2,1:T(8,128)S(1)} %get-tuple-element.159, f32[128,32,64]{0,2,1:T(8,128)S(1)} %get-tuple-element.158), kind=kLoop, calls=%fused_computation.49 | loop fusion | flops 524288 | bytes 4194304 | tf_op jit(solution)/shard_map/concatenate | solution.py:62
  62.6 2.9 %copy.160 = f32[1,128,4096]{2,1,0:T(8,128)} copy(f32[1,128,4096]{1,2,0:T(8,128)} %bitcast.227) | data formatting | bytes 4194304 | tf_op jit(solution)/shard_map/concatenate | solution.py:62
  65.5 3.0 %copy.106 = f32[1,128,4096]{2,1,0:T(8,128)} copy(f32[1,128,4096]{1,2,0:T(8,128)} %bitcast.226) | data formatting | bytes 4194304 | tf_op jit(solution)/shard_map/reshape | solution.py:181
  68.5 1.8 %copy.109 = f32[128,4,128]{0,2,1:T(8,128)} copy(f32[128,4,128]{2,0,1:T(8,128)} %get-tuple-element.79) | data formatting | bytes 524288 | tf_op jit(solution)/shard_map/cond | solution.py:161
  70.2 11.9 %collective-permute-start.5 = (f32[128,4,128]{0,2,1:T(8,128)}, f32[128,4,128]{0,2,1:T(8,128)S(1)}, u32[]{:S(2)}, u32[]{:S(2)}) collective-permute-start(f32[128,4,128]{0,2,1:T(8,128)} %copy.109), channel_id=1, source_target_pairs={{4,0},{8,4},{12,8},{16,12},{20,16},{24,20},{28,24},{32,28},{36,32}... | collective-permute-start | bytes 786440 | tf_op jit(solution)/shard_map/ppermute | solution.py:23
  82.1 1.8 %copy.110 = f32[128,4,128]{0,2,1:T(8,128)} copy(f32[128,4,128]{2,0,1:T(8,128)} %get-tuple-element.80) | data formatting | bytes 524288 | tf_op jit(solution)/shard_map/cond | solution.py:161
  83.9 2.0 %collective-permute-start.6 = (f32[128,4,128]{0,2,1:T(8,128)}, f32[128,4,128]{0,2,1:T(8,128)}, u32[]{:S(2)}, u32[]{:S(2)}) collective-permute-start(f32[128,4,128]{0,2,1:T(8,128)} %copy.110), channel_id=1, source_target_pairs={{8,0},{12,4},{16,8},{20,12},{24,16},{28,20},{32,24},{36,28},{40,32... | collective-permute-start | bytes 786440 | tf_op jit(solution)/shard_map/ppermute | solution.py:23
  85.9 4.2 %add_convert_fusion = bf16[1,128,4096]{2,1,0:T(8,128)(2,1)} fusion(f32[1,128,4096]{2,1,0:T(8,128)} %copy.160, f32[1,128,4096]{2,1,0:T(8,128)} %copy.106, f32[1,128,4096]{2,1,0:T(8,128)} %mul.242), kind=kLoop, calls=%fused_computation.67 | loop fusion | flops 1572864 | bytes 7340032 | tf_op jit(solution)/shard_map/convert_element_type | solution.py:182
  90.1 2.3 %collective-permute-start.4 = (bf16[1,128,4096]{2,1,0:T(8,128)(2,1)}, bf16[1,128,4096]{2,1,0:T(8,128)(2,1)}, u32[]{:S(2)}, u32[]{:S(2)}) collective-permute-start(bf16[1,128,4096]{2,1,0:T(8,128)(2,1)} %add_convert_fusion), channel_id=1, source_target_pairs={{1,0},{2,1},{3,2},{5,4},{6,5},{7,6},{9,8},{10,9},{11,10},{13,12},{... | collective-permute-start | bytes 3145736 | tf_op jit(solution)/shard_map/ppermute | solution.py:23
  92.5 1.8 %copy.112 = f32[128,4,128]{0,2,1:T(8,128)} copy(f32[128,4,128]{2,0,1:T(8,128)} %get-tuple-element.81) | data formatting | bytes 524288 | tf_op jit(solution)/shard_map/cond | solution.py:161
  94.3 1.9 %collective-permute-start.7 = (f32[128,4,128]{0,2,1:T(8,128)}, f32[128,4,128]{0,2,1:T(8,128)}, u32[]{:S(2)}, u32[]{:S(2)}) collective-permute-start(f32[128,4,128]{0,2,1:T(8,128)} %copy.112), channel_id=1, source_target_pairs={{4,0},{8,4},{12,8},{16,12},{20,16},{24,20},{28,24},{32,28},{36,32}... | collective-permute-start | bytes 786440 | tf_op jit(solution)/shard_map/ppermute | solution.py:23
  96.2 1.8 %copy.113 = f32[128,4,128]{0,2,1:T(8,128)} copy(f32[128,4,128]{2,0,1:T(8,128)} %get-tuple-element.82) | data formatting | bytes 524288 | tf_op jit(solution)/shard_map/cond | solution.py:161
  98.0 3.8 %collective-permute-start.8 = (f32[128,4,128]{0,2,1:T(8,128)}, f32[128,4,128]{0,2,1:T(8,128)}, u32[]{:S(2)}, u32[]{:S(2)}) collective-permute-start(f32[128,4,128]{0,2,1:T(8,128)} %copy.113), channel_id=1, source_target_pairs={{8,0},{12,4},{16,8},{20,12},{24,16},{28,20},{32,24},{36,28},{40,32... | collective-permute-start | bytes 786440 | tf_op jit(solution)/shard_map/ppermute | solution.py:23
  101.8 1.4 %broadcast_multiply_fusion = (f32[128,4,128]{0,2,1:T(8,128)S(1)}, f32[128,4,128]{0,2,1:T(8,128)S(1)}) fusion(f32[128,128]{0,1:T(8,128)S(1)} %get-tuple-element.167, f32[128,4,128]{0,2,1:T(8,128)S(1)} %collective-permute-done.5, f32[128,4,128]{0,2,1:T(8,128)} %collective-permute-done.6, bf16[128,4,8,128]{0,3,2,1:T(8,128)(2,1)S(1)} %fusion.33, ...), kind=kOutput, calls=%fused_computation.92 | convolution fusion | flops 134479872 | bytes 3211264 | tf_op jit(solution)/shard_map/tgru,tgre->uge/dot_general | solution.py:147
  103.2 1.0 fusion.54
  104.2 0.8 copy.114
  105.0 4.2 %collective-permute-done.8 = f32[128,4,128]{0,2,1:T(8,128)} collective-permute-done((f32[128,4,128]{0,2,1:T(8,128)}, f32[128,4,128]{0,2,1:T(8,128)}, u32[]{:S(2)}, u32[]{:S(2)}) %collective-permute-start.8) | collective-permute-done | bytes 262176 | tf_op jit(solution)/shard_map/ppermute | solution.py:23
  109.2 2.2 %add_convert_fusion.1 = bf16[128,4,128]{0,2,1:T(8,128)(2,1)S(1)} fusion(f32[128,4,128]{0,2,1:T(8,128)} %collective-permute-done.7, f32[128,4,128]{0,2,1:T(8,128)} %collective-permute-done.8, bf16[128,4,8,128]{0,3,2,1:T(8,128)(2,1)S(1)} %bitcast.223, f32[4,128,128,8]{2,1,3,0:T(8,128)} %copy-done, f32[128,4,8]{0,2,1:T(8,128)} %copy-done.9, ...), kind=kOutput, calls=%fused_computation.84 | convolution fusion | flops 136511488 | bytes 3833856 | tf_op jit(solution)/shard_map/tgru,tgre->uge/dot_general | solution.py:150
  111.4 0.8 copy.115
  112.2 5.2 %collective-permute-done.4 = bf16[1,128,4096]{2,1,0:T(8,128)(2,1)} collective-permute-done((bf16[1,128,4096]{2,1,0:T(8,128)(2,1)}, bf16[1,128,4096]{2,1,0:T(8,128)(2,1)}, u32[]{:S(2)}, u32[]{:S(2)}) %collective-permute-start.4) | collective-permute-done | bytes 1048608 | tf_op jit(solution)/shard_map/ppermute | solution.py:23
  117.4 2.3 %copy.186 = bf16[1,128,4096]{2,1,0:T(8,128)(2,1)} copy(bf16[1,128,4096]{2,1,0:T(8,128)(2,1)} %collective-permute-done.4) | data formatting | bytes 2097152
  (45 shorter events, 1.2 us)
Async XLA Ops:
  0.6 18.5 %copy-start.14 = (s32[1,2]{1,0:T(1,128)S(1)}, s32[1,2]{1,0:T(1,128)}, u32[]{:S(2)}) copy-start(s32[1,2]{1,0:T(1,128)} %param.21) | copy-start | bytes 28
  0.6 19.7 %copy-start.4 = (bf16[1,128,4096]{2,1,0:T(8,128)(2,1)S(1)}, bf16[1,128,4096]{2,1,0:T(8,128)(2,1)}, u32[]{:S(2)}) copy-start(bf16[1,128,4096]{2,1,0:T(8,128)(2,1)} %param.15) | copy-start | bytes 3145732
  3.5 30.7 %collective-permute-start.1 = (bf16[128,4,128]{0,2,1:T(8,128)(2,1)}, bf16[128,4,128]{0,2,1:T(8,128)(2,1)S(1)}, u32[]{:S(2)}, u32[]{:S(2)}) collective-permute-start(bf16[128,4,128]{0,2,1:T(8,128)(2,1)} %fusion.53), channel_id=1, source_target_pairs={{0,8},{4,12},{8,16},{12,20},{16,24},{20,28},{24,32},{28,36},{32,40... | collective-permute-start | bytes 393224 | tf_op jit(solution)/shard_map/ppermute | solution.py:23
  7.3 27.5 %collective-permute-start = (bf16[128,4,128]{0,2,1:T(8,128)(2,1)}, bf16[128,4,128]{0,2,1:T(8,128)(2,1)S(1)}, u32[]{:S(2)}, u32[]{:S(2)}) collective-permute-start(bf16[128,4,128]{0,2,1:T(8,128)(2,1)} %fusion.53), channel_id=1, source_target_pairs={{0,4},{4,8},{8,12},{12,16},{16,20},{20,24},{24,28},{28,32},{32,36}... | collective-permute-start | bytes 393224 | tf_op jit(solution)/shard_map/ppermute | solution.py:23
  10.9 32.0 %collective-permute-start.3 = (bf16[128,4,128]{0,2,1:T(8,128)(2,1)}, bf16[128,4,128]{0,2,1:T(8,128)(2,1)}, u32[]{:S(2)}, u32[]{:S(2)}) collective-permute-start(bf16[128,4,128]{0,2,1:T(8,128)(2,1)} %bitcast.37), channel_id=1, source_target_pairs={{0,8},{4,12},{8,16},{12,20},{16,24},{20,28},{24,32},{28,36},{32,40... | collective-permute-start | bytes 393224 | tf_op jit(solution)/shard_map/ppermute | solution.py:23
  14.7 31.3 %collective-permute-start.2 = (bf16[128,4,128]{0,2,1:T(8,128)(2,1)}, bf16[128,4,128]{0,2,1:T(8,128)(2,1)}, u32[]{:S(2)}, u32[]{:S(2)}) collective-permute-start(bf16[128,4,128]{0,2,1:T(8,128)(2,1)} %bitcast.37), channel_id=1, source_target_pairs={{0,4},{4,8},{8,12},{12,16},{16,20},{20,24},{24,28},{28,32},{32,36}... | collective-permute-start | bytes 393224 | tf_op jit(solution)/shard_map/ppermute | solution.py:23
  21.2 2.0 %copy-start.1 = (f32[1,128,4096]{1,2,0:T(8,128)}, f32[1,128,4096]{1,2,0:T(8,128)S(1)}, u32[]{:S(2)}) copy-start(f32[1,128,4096]{1,2,0:T(8,128)S(1)} %convert_element_type.119) | copy-start | bytes 6291460
  21.2 2.7 %copy-start.5 = (bf16[1,128,4096]{2,1,0:T(8,128)(2,1)S(1)}, bf16[1,128,4096]{2,1,0:T(8,128)(2,1)}, u32[]{:S(2)}) copy-start(bf16[1,128,4096]{2,1,0:T(8,128)(2,1)} %param.19) | copy-start | bytes 3145732
  23.2 1.4 %copy-start.6 = (bf16[1,128,4096]{2,1,0:T(8,128)(2,1)S(1)}, bf16[1,128,4096]{2,1,0:T(8,128)(2,1)}, u32[]{:S(2)}) copy-start(bf16[1,128,4096]{2,1,0:T(8,128)(2,1)} %param.18) | copy-start | bytes 3145732
  26.9 1.5 %copy-start.13 = (s32[128]{0:T(128)S(1)}, s32[128]{0:T(128)}, u32[]{:S(2)}) copy-start(s32[128]{0:T(128)} %param.20) | copy-start | bytes 1540
  28.6 4.2 %copy-start.7 = (pred[128,128]{0,1:T(8,128)(4,1)}, pred[128,128]{0,1:T(8,128)(4,1)S(1)}, u32[]{:S(2)}) copy-start(pred[128,128]{0,1:T(8,128)(4,1)S(1)} %get-tuple-element.168) | copy-start | bytes 49156
  28.6 5.6 %copy-start.11 = (pred[128,128]{0,1:T(8,128)(4,1)}, pred[128,128]{0,1:T(8,128)(4,1)S(1)}, u32[]{:S(2)}) copy-start(pred[128,128]{0,1:T(8,128)(4,1)S(1)} %get-tuple-element.170) | copy-start | bytes 49156
  28.6 6.2 %copy-start.10 = (pred[128,128]{0,1:T(8,128)(4,1)}, pred[128,128]{0,1:T(8,128)(4,1)S(1)}, u32[]{:S(2)}) copy-start(pred[128,128]{0,1:T(8,128)(4,1)S(1)} %get-tuple-element.169) | copy-start | bytes 49156
  31.3 2.0 %copy-start.3 = (bf16[1,128,4096]{1,2,0:T(8,128)(2,1)S(1)}, bf16[1,128,4096]{1,2,0:T(8,128)(2,1)}, u32[]{:S(2)}) copy-start(bf16[1,128,4096]{1,2,0:T(8,128)(2,1)} %copy.93) | copy-start | bytes 3145732
  32.8 1.3 %copy-start = (f32[4,128,128,8]{2,1,3,0:T(8,128)}, f32[4,128,128,8]{2,1,3,0:T(8,128)S(1)}, u32[]{:S(2)}) copy-start(f32[4,128,128,8]{2,1,3,0:T(8,128)S(1)} %get-tuple-element.174) | copy-start | bytes 6291460
  37.9 5.0 %copy-start.9 = (f32[128,4,8]{0,2,1:T(8,128)}, f32[128,4,8]{0,2,1:T(8,128)S(1)}, u32[]{:S(2)}) copy-start(f32[128,4,8]{0,2,1:T(8,128)S(1)} %log_add_fusion) | copy-start | bytes 49156
  40.2 2.7 %copy-start.12 = (pred[128,128]{0,1:T(8,128)(4,1)S(1)}, pred[128,128]{0,1:T(8,128)(4,1)}, u32[]{:S(2)}) copy-start(pred[128,128]{0,1:T(8,128)(4,1)} %copy-done.11) | copy-start | bytes 49156
  59.4 1.4 %copy-start.2 = (f32[128,4,8,128]{0,3,2,1:T(8,128)}, f32[128,4,8,128]{0,3,2,1:T(8,128)S(1)}, u32[]{:S(2)}) copy-start(f32[128,4,8,128]{0,3,2,1:T(8,128)S(1)} %fusion.35) | copy-start | bytes 6291460
  70.2 31.5 %collective-permute-start.5 = (f32[128,4,128]{0,2,1:T(8,128)}, f32[128,4,128]{0,2,1:T(8,128)S(1)}, u32[]{:S(2)}, u32[]{:S(2)}) collective-permute-start(f32[128,4,128]{0,2,1:T(8,128)} %copy.109), channel_id=1, source_target_pairs={{4,0},{8,4},{12,8},{16,12},{20,16},{24,20},{28,24},{32,28},{36,32}... | collective-permute-start | bytes 786440 | tf_op jit(solution)/shard_map/ppermute | solution.py:23
  83.9 17.8 %collective-permute-start.6 = (f32[128,4,128]{0,2,1:T(8,128)}, f32[128,4,128]{0,2,1:T(8,128)}, u32[]{:S(2)}, u32[]{:S(2)}) collective-permute-start(f32[128,4,128]{0,2,1:T(8,128)} %copy.110), channel_id=1, source_target_pairs={{8,0},{12,4},{16,8},{20,12},{24,16},{28,20},{32,24},{36,28},{40,32... | collective-permute-start | bytes 786440 | tf_op jit(solution)/shard_map/ppermute | solution.py:23
  90.1 27.3 %collective-permute-start.4 = (bf16[1,128,4096]{2,1,0:T(8,128)(2,1)}, bf16[1,128,4096]{2,1,0:T(8,128)(2,1)}, u32[]{:S(2)}, u32[]{:S(2)}) collective-permute-start(bf16[1,128,4096]{2,1,0:T(8,128)(2,1)} %add_convert_fusion), channel_id=1, source_target_pairs={{1,0},{2,1},{3,2},{5,4},{6,5},{7,6},{9,8},{10,9},{11,10},{13,12},{... | collective-permute-start | bytes 3145736 | tf_op jit(solution)/shard_map/ppermute | solution.py:23
  94.3 10.7 %collective-permute-start.7 = (f32[128,4,128]{0,2,1:T(8,128)}, f32[128,4,128]{0,2,1:T(8,128)}, u32[]{:S(2)}, u32[]{:S(2)}) collective-permute-start(f32[128,4,128]{0,2,1:T(8,128)} %copy.112), channel_id=1, source_target_pairs={{4,0},{8,4},{12,8},{16,12},{20,16},{24,20},{28,24},{32,28},{36,32}... | collective-permute-start | bytes 786440 | tf_op jit(solution)/shard_map/ppermute | solution.py:23
  98.0 11.2 %copy-start.8 = (pred[128,128]{0,1:T(8,128)(4,1)S(1)}, pred[128,128]{0,1:T(8,128)(4,1)}, u32[]{:S(2)}) copy-start(pred[128,128]{0,1:T(8,128)(4,1)} %copy-done.7) | copy-start | bytes 49156
  98.0 11.2 %collective-permute-start.8 = (f32[128,4,128]{0,2,1:T(8,128)}, f32[128,4,128]{0,2,1:T(8,128)}, u32[]{:S(2)}, u32[]{:S(2)}) collective-permute-start(f32[128,4,128]{0,2,1:T(8,128)} %copy.113), channel_id=1, source_target_pairs={{8,0},{12,4},{16,8},{20,12},{24,16},{28,20},{32,24},{36,28},{40,32... | collective-permute-start | bytes 786440 | tf_op jit(solution)/shard_map/ppermute | solution.py:23
where the time goes:
time: 121 us; the launch traced here: 120 us
  starting transfers between devices  35.1 us (29%)
  local copies, waits for them, and re-layouts  34.9 us (29%)
  other arithmetic  19.6 us (16%)
  matrix products  18.2 us (15%)
  waiting for transfers between devices  9.42 us (8%)
  between operations  2.4 us (2%)
    ppermute x9, starting transfers between devices, from_behind(): lax.ppermute(value, axis, [(source, source + steps) for source in range(i...  35.1 us
    unnamed x37, local copies, waits for them, and re-layouts  10.3 us
    cond x5, local copies, waits for them, and re-layouts, shards(): lax.cond(listed[distance - 1] == 1, lambda k_blk=blocks[distance][0], v_b...  10.1 us
    ppermute x9, waiting for transfers between devices, from_behind(): lax.ppermute(value, axis, [(source, source + steps) for source in range(i...  9.42 us
    dot_general x2, matrix products, tile_grads(): jnp.einsum('tgru,uge->tgre', dscore, k_blk, preferred_element_type=jnp.fl...  4.57 us
    convert_element_type x1, other arithmetic, shards(): query_grad = undo_rope(dq_sum.reshape(tok_rows, HQ, HD), cosine, sine_tab...  4.17 us
    dot_general x2, matrix products, tile_grads(): jnp.einsum('tgre,uge->tgru', grad_rows, v_blk, preferred_element_type=jnp...  3.75 us
    dot_general x2, matrix products, tile_grads(): jnp.einsum('tgru,tgre->uge', prob_b, grad_rows, preferred_element_type=jn...  3.42 us
  transfers between devices with their start and end apart: 9, of which 2 were waited for; matrix products, arithmetic and copies ran while one was open for 35% of the time, Pallas kernels for 0%

commit v1 on v0

v1 whole, which is shorter than its diff:
```python
import functools
import math

import jax
import jax.numpy as jnp
import numpy as np
from jax import lax
from jax.experimental import pallas as pl
from jax.experimental.pallas import tpu as pltpu
from jax.sharding import PartitionSpec as P

HQ = 32
HK = 4
HD = 128
TOK = 128
RATIO = HQ // HK
PAIRS = RATIO // 2
HALF = HD // 2
ROPE_BASE = 1000000.0
TRAINED_CONTEXT = 32768.0
YARN_FACTOR = 4.0
NEG_LARGE = -1.0e30
SCALE = HD**-0.5
LONG = 0
MESH = pl.DeviceIdType.MESH
F32 = jnp.float32
BF16 = jnp.bfloat16


def yarn_frequencies():
    def correction(rotations):
        return HD * math.log(TRAINED_CONTEXT / (rotations * 2.0 * math.pi)) / (2.0 * math.log(ROPE_BASE))

    lower = max(math.floor(correction(32.0)), 0)
    upper = min(math.ceil(correction(1.0)), HD - 1)
    spread = max(upper - lower, 0.001)
    index = np.arange(HALF, dtype=np.float64)
    base = ROPE_BASE ** (-2.0 * index / HD)
    ramp = np.clip((index - lower) / spread, 0.0, 1.0)
    return (base / YARN_FACTOR * ramp + base * (1.0 - ramp)).astype(np.float32)


def sin_cos(x):
    n = jnp.floor(x * (2.0 / math.pi) + 0.5)
    r = x - n * 1.5703125
    r = r - n * 4.83751296997070312e-4
    r = r - n * 7.54978995489188216e-8
    z = r * r
    sin = r + r * z * (-1.6666654611e-1 + z * (8.3321608736e-3 + z * -1.9515295891e-4))
    cos = 1.0 - 0.5 * z + z * z * (4.166664568298827e-2 + z * (-1.388731625493765e-3 + z * 2.443315711809948e-5))
    q = n.astype(jnp.int32) & 3
    odd = (q & 1) == 1
    s = jnp.where(odd, cos, sin)
    c = jnp.where(odd, sin, cos)
    return jnp.where(q >= 2, -s, s), jnp.where((q == 1) | (q == 2), -c, c)


def dot_t(a, b):
    return lax.dot_general(a, b, (((1,), (1,)), ((), ())), preferred_element_type=F32)


def dot(a, b):
    return jnp.dot(a, b, preferred_element_type=F32)


def kernel(
    n_ctx,
    doc_ref, fetch_ref, freq_ref, q_hbm, k_hbm, v_hbm, o_hbm, do_hbm,
    out_ref, dk_ref, dv_ref,
    q_in, k_in, o_in, do_in,
    kv, qr, doz, bias, tab_t, tab_c, tab_s, k_t, p_win, ds_win, own, back_out, back_in, dq, relay,
    in_sem, kv_send, kv_recv, back_send, back_recv, dq_send, out_recv, relay_recv, relay_send,
):
    c = lax.axis_index("ctx")
    s = lax.axis_index("section")

    loads = [pltpu.make_async_copy(k_hbm.at[0], k_in, in_sem.at[0])]
    for g in range(HK):
        loads.append(pltpu.make_async_copy(v_hbm.at[0, :, pl.ds(g * HD, HD)], kv.at[0, g, 1], in_sem.at[1 + g]))
    loads.append(pltpu.make_async_copy(q_hbm.at[0], q_in, in_sem.at[5]))
    loads.append(pltpu.make_async_copy(do_hbm.at[0], do_in, in_sem.at[6]))
    loads.append(pltpu.make_async_copy(o_hbm.at[0], o_in, in_sem.at[7]))
    for load in loads:
        load.start()

    barrier = pltpu.get_barrier_semaphore()
    for d in (1, 2):
        @pl.when(c >= d)
        def _():
            pl.semaphore_signal(barrier, inc=1, device_id=(c - d, s), device_id_type=MESH)
    for me, others in ((0, (1, 2, 3)), (1, (0, 2)), (2, (0, 1, 3))):
        @pl.when(s == me)
        def _():
            for other in others:
                pl.semaphore_signal(barrier, inc=1, device_id=(c, other), device_id_type=MESH)

    first = c * TOK
    lane_t = lax.broadcasted_iota(jnp.int32, (1, TOK), 1) + first
    start = doc_ref[...]
    factor = 0.1 * math.log(YARN_FACTOR) + 1.0
    sin, cos = sin_cos((lane_t - start).astype(F32) * freq_ref[...])
    sin = sin * factor
    cos = cos * factor
    tab_t[0] = cos * SCALE
    tab_t[1] = sin * SCALE
    turned = jnp.concatenate([cos, sin], axis=0).T
    swapped = pltpu.roll(turned, HALF, 1)
    low = lax.broadcasted_iota(jnp.int32, (TOK, HD), 1) < HALF
    tab_c[...] = jnp.where(low, turned, swapped)
    tab_s[...] = jnp.where(low, -swapped, turned)

    def rope(x):
        x = x.astype(F32)
        return (x * tab_c[...] + pltpu.roll(x, HALF, 1) * tab_s[...]).astype(BF16)

    loads[0].wait()
    for g in range(HK):
        kv[0, g, 0] = rope(k_in[:, g * HD : (g + 1) * HD])
    for g in range(HK):
        loads[1 + g].wait()

    pl.semaphore_wait(
        barrier, 2 + (c < n_ctx - 1).astype(jnp.int32) + (c < n_ctx - 2).astype(jnp.int32)
    )

    def kv_copy(g, d):
        return pltpu.make_async_remote_copy(
            src_ref=kv.at[0, g], dst_ref=kv.at[d, g],
            send_sem=kv_send.at[d - 1, g], recv_sem=kv_recv.at[d - 1, g],
            device_id=(c + d, s), device_id_type=MESH,
        )

    for g in range(HK):
        for d in (1, 2):
            pl.when(c < n_ctx - d)(kv_copy(g, d).start)
    for d in (1, 2):
        @pl.when(c < d)
        def _():
            kv[d] = jnp.zeros((HK, 2, TOK, HD), BF16)
        @pl.when(c >= n_ctx - d)
        def _():
            back_in[d - 1] = jnp.zeros((HK, 2, TOK, HD), BF16)

    def zero_copy(p):
        return pltpu.make_async_copy(
            relay.at[0, 0], out_ref.at[0, :, pl.ds(pl.multiple_of(p * 2 * HD, 2 * HD), 2 * HD)], out_recv.at[p]
        )

    @pl.when(s == 3)
    def _():
        relay[0, 0] = jnp.zeros((TOK, 2 * HD), BF16)

        def put(p, carry):
            zero_copy(p).start()
            return carry

        lax.fori_loop(0, HK * PAIRS, put, 0)

    row = lax.broadcasted_iota(jnp.int32, (TOK, TOK), 0)
    for d in range(3):
        u = first - d * TOK + row
        allowed = (u >= start) & (u <= lane_t)
        if d > 0:
            allowed = allowed & (fetch_ref[:, d - 1 : d] == 1)
        bias[d * TOK : (d + 1) * TOK, :] = jnp.where(allowed, 0.0, NEG_LARGE)

    loads[5].wait()
    loads[6].wait()
    loads[7].wait()

    def prepare(h, carry):
        cols = pl.ds(pl.multiple_of(h * HD, HD), HD)
        qr[h] = rope(q_in[:, cols])
        grad = do_in[:, cols]
        prod = grad.astype(F32) * o_in[:, cols].astype(F32)
        prod = prod + pltpu.roll(prod, HALF, 1)
        high = prod.astype(BF16).astype(F32)
        doz[h, :, 0:HD] = grad
        doz[h, :, HD : 2 * HD] = jnp.where(low, high, prod - high).astype(BF16)
        return carry

    lax.fori_loop(0, HQ, prepare, 0)

    def out_cols(p):
        return out_ref.at[0, :, pl.ds(pl.multiple_of(p * 2 * HD, 2 * HD), 2 * HD)]

    def direct_copy(p):
        return pltpu.make_async_remote_copy(
            src_ref=dq.at[p], dst_ref=out_cols(p), send_sem=dq_send.at[p], recv_sem=out_recv.at[p],
            device_id=(c, s - 1), device_id_type=MESH,
        )

    def long_copy(g):
        return pltpu.make_async_remote_copy(
            src_ref=dq.at[g * PAIRS + LONG], dst_ref=relay.at[s // 3, g],
            send_sem=dq_send.at[g * PAIRS + LONG], recv_sem=relay_recv.at[s // 3, g],
            device_id=(c, 2 * (1 - s // 2)), device_id_type=MESH,
        )

    def relay_copy(slot, g, target):
        p = g * PAIRS + LONG
        return pltpu.make_async_remote_copy(
            src_ref=relay.at[slot, g], dst_ref=out_cols(p),
            send_sem=relay_send.at[slot, g], recv_sem=out_recv.at[p],
            device_id=(c, target), device_id_type=MESH,
        )

    def arrival(slot, g):
        return pltpu.make_async_remote_copy(
            src_ref=dq.at[g * PAIRS + LONG], dst_ref=relay.at[slot, g],
            send_sem=dq_send.at[g * PAIRS + LONG], recv_sem=relay_recv.at[slot, g],
            device_id=(c, 0), device_id_type=MESH,
        )

    def forward(g):
        @pl.when(s == 0)
        def _():
            arrival(0, g).wait_recv()
            relay_copy(0, g, 1).start()
            arrival(1, g).wait_recv()
            relay_copy(1, g, 2).start()

        @pl.when(s == 2)
        def _():
            arrival(0, g).wait_recv()
            relay_copy(0, g, 0).start()

    def back_copy(g, d):
        return pltpu.make_async_remote_copy(
            src_ref=back_out.at[d - 1, g], dst_ref=back_in.at[d - 1, g],
            send_sem=back_send.at[d - 1, g], recv_sem=back_recv.at[d - 1, g],
            device_id=(c - d, s), device_id_type=MESH,
        )

    def group(g, carry):
        for d in (1, 2):
            pl.when(c >= d)(kv_copy(g, d).wait_recv)
        k_win = jnp.concatenate([kv[d, g, 0] for d in range(3)], axis=0)
        v_win = jnp.concatenate([kv[d, g, 1] for d in range(3)], axis=0)
        v_one = jnp.concatenate([v_win, jnp.full((3 * TOK, HD), -1.0, BF16)], axis=1)
        k_t[...] = k_win.T
        for j in range(PAIRS):
            p = g * PAIRS + j
            h = g * RATIO + 2 * j
            qp = qr[pl.ds(h, 2)].reshape(2 * TOK, HD)
            dp_in = doz[pl.ds(h, 2)].reshape(2 * TOK, 2 * HD)
            sc = dot_t(k_win, qp) * (SCALE * math.log2(math.e))
            b = bias[...]
            sc = sc + jnp.concatenate([b, b], axis=1)
            e = jnp.exp2(sc - jnp.max(sc, axis=0, keepdims=True))
            prob = e * (1.0 / jnp.sum(e, axis=0, keepdims=True))
            ds = (prob * dot_t(v_one, dp_in)).astype(BF16)
            p_win[:, 2 * j * TOK : 2 * (j + 1) * TOK] = prob.astype(BF16)
            ds_win[:, 2 * j * TOK : 2 * (j + 1) * TOK] = ds
            turned_grad = dot(k_t[...], ds)
            for i in range(2):
                x = turned_grad[:HALF, i * TOK : (i + 1) * TOK]
                y = turned_grad[HALF:, i * TOK : (i + 1) * TOK]
                grad = jnp.concatenate(
                    [x * tab_t[0] + y * tab_t[1], y * tab_t[0] - x * tab_t[1]], axis=0
                )
                dq[p, :, i * HD : (i + 1) * HD] = grad.T.astype(BF16)

            @pl.when(s >= 1)
            def _():
                if j == LONG:
                    long_copy(g).start()
                else:
                    direct_copy(p).start()

        dk = dot(ds_win[...], qr[pl.ds(g * RATIO, RATIO)].reshape(RATIO * TOK, HD))
        dv = dot(p_win[...], doz[pl.ds(g * RATIO, RATIO), :, 0:HD].reshape(RATIO * TOK, HD))
        own[g, 0] = dk[:TOK]
        own[g, 1] = dv[:TOK]
        for d in (1, 2):
            back_out[d - 1, g, 0] = dk[d * TOK : (d + 1) * TOK].astype(BF16)
            back_out[d - 1, g, 1] = dv[d * TOK : (d + 1) * TOK].astype(BF16)
            pl.when(c >= d)(back_copy(g, d).start)

        @pl.when(g >= 1)
        def _():
            forward(g - 1)

        return carry

    lax.fori_loop(0, HK, group, 0)
    forward(HK - 1)

    def finish(g, carry):
        for d in (1, 2):
            pl.when(c < n_ctx - d)(back_copy(g, d).wait_recv)
        dk = own[g, 0] + back_in[0, g, 0].astype(F32) + back_in[1, g, 0].astype(F32)
        dv = own[g, 1] + back_in[0, g, 1].astype(F32) + back_in[1, g, 1].astype(F32)
        dk = dk * SCALE
        cols = pl.ds(pl.multiple_of(g * HD, HD), HD)
        dk_ref[0, :, cols] = (dk * tab_c[...] - pltpu.roll(dk, HALF, 1) * tab_s[...]).astype(BF16)
        dv_ref[0, :, cols] = dv.astype(BF16)
        return carry

    lax.fori_loop(0, HK, finish, 0)

    def drain(g, carry):
        for d in (1, 2):
            pl.when(c < n_ctx - d)(kv_copy(g, d).wait_send)
            pl.when(c >= d)(back_copy(g, d).wait_send)

        @pl.when(s >= 1)
        def _():
            for j in range(PAIRS):
                direct_copy(g * PAIRS + j).wait_send()

        @pl.when(s == 0)
        def _():
            relay_copy(0, g, 1).wait_send()
            relay_copy(1, g, 2).wait_send()

        @pl.when(s == 2)
        def _():
            relay_copy(0, g, 0).wait_send()

        @pl.when(s <= 2)
        def _():
            for j in range(PAIRS):
                direct_copy(g * PAIRS + j).wait_recv()

        @pl.when(s == 3)
        def _():
            for j in range(PAIRS):
                zero_copy(g * PAIRS + j).wait()

        return carry

    lax.fori_loop(0, HK, drain, 0)


def solution(mesh):
    n_ctx = mesh.shape["ctx"]
    freq = np.broadcast_to(yarn_frequencies()[:, None], (HALF, TOK)).copy()

    def shards(q, k, v, o, do, doc_start, fetch_list):
        any_spec = pl.BlockSpec(memory_space=pl.ANY)
        vmem = pl.BlockSpec(memory_space=pltpu.VMEM)
        dma = pltpu.SemaphoreType.DMA
        return pl.pallas_call(
            functools.partial(kernel, n_ctx),
            out_shape=(
                jax.ShapeDtypeStruct((1, TOK, HQ * HD), BF16),
                jax.ShapeDtypeStruct((1, TOK, HK * HD), BF16),
                jax.ShapeDtypeStruct((1, TOK, HK * HD), BF16),
            ),
            in_specs=[vmem] * 3 + [any_spec] * 5,
            out_specs=(any_spec, vmem, vmem),
            scratch_shapes=[
                pltpu.VMEM((TOK, HQ * HD), BF16),
                pltpu.VMEM((TOK, HK * HD), BF16),
                pltpu.VMEM((TOK, HQ * HD), BF16),
                pltpu.VMEM((TOK, HQ * HD), BF16),
                pltpu.VMEM((3, HK, 2, TOK, HD), BF16),
                pltpu.VMEM((HQ, TOK, HD), BF16),
                pltpu.VMEM((HQ, TOK, 2 * HD), BF16),
                pltpu.VMEM((3 * TOK, TOK), F32),
                pltpu.VMEM((2, HALF, TOK), F32),
                pltpu.VMEM((TOK, HD), F32),
                pltpu.VMEM((TOK, HD), F32),
                pltpu.VMEM((HD, 3 * TOK), BF16),
                pltpu.VMEM((3 * TOK, RATIO * TOK), BF16),
                pltpu.VMEM((3 * TOK, RATIO * TOK), BF16),
                pltpu.VMEM((HK, 2, TOK, HD), F32),
                pltpu.VMEM((2, HK, 2, TOK, HD), BF16),
                pltpu.VMEM((2, HK, 2, TOK, HD), BF16),
                pltpu.VMEM((HK * PAIRS, TOK, 2 * HD), BF16),
                pltpu.VMEM((2, HK, TOK, 2 * HD), BF16),
                dma((8,)),
                dma((2, HK)),
                dma((2, HK)),
                dma((2, HK)),
                dma((2, HK)),
                dma((HK * PAIRS,)),
                dma((HK * PAIRS,)),
                dma((2, HK)),
                dma((2, HK)),
            ],
            compiler_params=pltpu.CompilerParams(
                collective_id=0, has_side_effects=True, vmem_limit_bytes=24 << 20
            ),
            cost_estimate=pl.CostEstimate(flops=2_000_000_000, bytes_accessed=5_000_000, transcendentals=1_600_000),
        )(doc_start.reshape(1, TOK), fetch_list, jnp.asarray(freq), q, k, v, o, do)

    return jax.shard_map(
        shards,
        mesh=mesh,
        in_specs=(
            P("section", "ctx", None),
            P("section", "ctx", None),
            P("section", "ctx", None),
            P("section", "ctx", None),
            P("section", "ctx", None),
            P("ctx"),
            P("ctx", None),
        ),
        out_specs=(P("section", "ctx", None),) * 3,
        check_vma=False,
    )
```

time: 121 us -> 45.9 us (0.38)
  Pallas kernels: 0 us -> 35.4 us
  starting transfers between devices: 35.1 us -> 0 us
  local copies, waits for them, and re-layouts: 34.9 us -> 9.18 us
  other arithmetic: 19.6 us -> 0 us
  matrix products: 18.2 us -> 0 us
  waiting for transfers between devices: 9.42 us -> 0 us
  between operations: 2.4 us -> 0.66 us
    pallas_call x0 -> x1, Pallas kernels: none -> 35.4 us  [shards(): pl.pallas_call(functools.partial(kernel, n_ctx), out_shape=(jax.ShapeDtyp...]
    ppermute x9 -> x0, starting transfers between devices: 35.1 us -> none  [from_behind(): lax.ppermute(value, axis, [(source, source + steps) for source in range(i...]
    dot_general x11 -> x0, matrix products: 18.2 us -> none  [the longest x2 4.57 us: tile_grads(): jnp.einsum('tgru,uge->tgre', dscore, k_blk, preferred_element_type=jnp.fl...]
    cond x5 -> x0, local copies, waits for them, and re-layouts: 10.1 us -> none  [shards(): lax.cond(listed[distance - 1] == 1, lambda k_blk=blocks[distance][0], v_b...]
    ppermute x9 -> x0, waiting for transfers between devices: 9.42 us -> none  [from_behind(): lax.ppermute(value, axis, [(source, source + steps) for source in range(i...]
    convert_element_type x6 -> x0, other arithmetic: 9.35 us -> none  [the longest x1 4.17 us: shards(): query_grad = undo_rope(dq_sum.reshape(tok_rows, HQ, HD), cosine, sine_tab...]
    add x4 -> x0, other arithmetic: 4.19 us -> none  [the longest x1 3.4 us: shards(): dq_sum = dq_sum + tile_result[0]]
    broadcast_in_dim x5 -> x0, local copies, waits for them, and re-layouts: 3.69 us -> none  [the longest x1 1.64 us: shards(): jnp.zeros((tok_rows, HK, ratio, HD), jnp.float32)]
  transfers between devices with their start and end apart: 9 -> 0, of which waited for: 2 -> 0; matrix products, arithmetic and copies ran while one was open for 35% -> 0% of each run, Pallas kernels for 0% -> 0%
where the time goes in v1:
time: 45.9 us; the launch traced here: 45.3 us
  Pallas kernels  35.4 us (77%)
  local copies, waits for them, and re-layouts  9.18 us (20%)
  between operations  0.66 us (1%)
    pallas_call x1, Pallas kernels, shards(): pl.pallas_call(functools.partial(kernel, n_ctx), out_shape=(jax.ShapeDtyp...  35.4 us
    unnamed x19, local copies, waits for them, and re-layouts  9.18 us

profile of v1, /device:TPU:20, one launch (start us, length us, event | category | flops | bytes accessed | tf_op | source)
XLA Modules:
  0.0 45.3 jit_solution(2705224347781512212)
XLA Ops:
  0.6 0.0 copy-start.6
  0.6 0.0 copy-start.5
  0.7 0.6 %copy-done.6 = s32[1,2]{1,0:T(1,128)S(1)} copy-done((s32[1,2]{1,0:T(1,128)S(1)}, s32[1,2]{1,0:T(1,128)}, u32[]{:S(2)}) %copy-start.6) | copy-done | bytes 32
  1.3 0.0 copy-done.5
  1.3 0.0 copy-start
  1.3 1.2 %copy-done = bf16[1,128,4096]{2,1,0:T(8,128)(2,1)S(1)} copy-done((bf16[1,128,4096]{2,1,0:T(8,128)(2,1)S(1)}, bf16[1,128,4096]{2,1,0:T(8,128)(2,1)}, u32[]{:S(2)}) %copy-start) | copy-done | bytes 1048600
  2.5 0.0 copy-start.1
  2.5 1.2 %copy-done.1 = bf16[1,128,4096]{2,1,0:T(8,128)(2,1)S(1)} copy-done((bf16[1,128,4096]{2,1,0:T(8,128)(2,1)S(1)}, bf16[1,128,4096]{2,1,0:T(8,128)(2,1)}, u32[]{:S(2)}) %copy-start.1) | copy-done | bytes 1048600
  3.8 0.0 copy-start.2
  3.8 1.2 %copy-done.2 = bf16[1,128,4096]{2,1,0:T(8,128)(2,1)S(1)} copy-done((bf16[1,128,4096]{2,1,0:T(8,128)(2,1)S(1)}, bf16[1,128,4096]{2,1,0:T(8,128)(2,1)}, u32[]{:S(2)}) %copy-start.2) | copy-done | bytes 1048600
  5.0 0.0 copy-start.3
  5.0 0.9 %copy-done.3 = bf16[1,128,512]{2,1,0:T(8,128)(2,1)S(1)} copy-done((bf16[1,128,512]{2,1,0:T(8,128)(2,1)S(1)}, bf16[1,128,512]{2,1,0:T(8,128)(2,1)}, u32[]{:S(2)}) %copy-start.3) | copy-done | bytes 131096
  5.9 0.0 copy-start.4
  5.9 0.9 %copy-done.4 = bf16[1,128,512]{2,1,0:T(8,128)(2,1)S(1)} copy-done((bf16[1,128,512]{2,1,0:T(8,128)(2,1)S(1)}, bf16[1,128,512]{2,1,0:T(8,128)(2,1)}, u32[]{:S(2)}) %copy-start.4) | copy-done | bytes 131096
  6.8 0.0 copy-start.7
  6.8 0.8 %copy-done.7 = f32[64,128]{1,0:T(8,128)S(1)} copy-done((f32[64,128]{1,0:T(8,128)S(1)}, f32[64,128]{1,0:T(8,128)}, u32[]{:S(2)}) %copy-start.7) | copy-done | bytes 32792
  7.5 35.4 %shard_map.103 = (bf16[1,128,4096]{2,1,0:T(8,128)(2,1)S(1)}, bf16[1,128,512]{2,1,0:T(8,128)(2,1)S(1)}, bf16[1,128,512]{2,1,0:T(8,128)(2,1)S(1)}) custom-call(s32[1,128]{1,0:T(1,128)S(1)} %bitcast.1, s32[1,2]{1,0:T(1,128)S(1)} %copy-done.6, f32[64,128]{1,0:T(8,128)S(1)} %copy-done.7, bf16[1,128,4096]{2,1,0:T(8,128)(2,1)S(1)} %copy-done, ...), custom_call_target="tpu_custom_call" | custom-call | flops 2000000000 | bytes 5000000 | tf_op jit(solution)/shard_map/pallas_call | solution.py:344
  43.0 1.0 %copy.14 = bf16[1,128,4096]{2,1,0:T(8,128)(2,1)} copy(bf16[1,128,4096]{2,1,0:T(8,128)(2,1)S(1)} %get-tuple-element.6) | data formatting | bytes 2097152
  43.9 0.7 %copy.15 = bf16[1,128,512]{2,1,0:T(8,128)(2,1)} copy(bf16[1,128,512]{2,1,0:T(8,128)(2,1)S(1)} %get-tuple-element.7) | data formatting | bytes 262144
  44.6 0.7 %copy.16 = bf16[1,128,512]{2,1,0:T(8,128)(2,1)} copy(bf16[1,128,512]{2,1,0:T(8,128)(2,1)S(1)} %get-tuple-element.8) | data formatting | bytes 262144
Async XLA Ops:
  0.6 0.7 %copy-start.6 = (s32[1,2]{1,0:T(1,128)S(1)}, s32[1,2]{1,0:T(1,128)}, u32[]{:S(2)}) copy-start(s32[1,2]{1,0:T(1,128)} %fetch_ref.1) | copy-start | bytes 28
  0.6 0.7 %copy-start.5 = (s32[128]{0:T(128)S(1)}, s32[128]{0:T(128)}, u32[]{:S(2)}) copy-start(s32[128]{0:T(128)} %param.13) | copy-start | bytes 1540
  1.3 1.2 %copy-start = (bf16[1,128,4096]{2,1,0:T(8,128)(2,1)S(1)}, bf16[1,128,4096]{2,1,0:T(8,128)(2,1)}, u32[]{:S(2)}) copy-start(bf16[1,128,4096]{2,1,0:T(8,128)(2,1)} %q_hbm.1) | copy-start | bytes 3145732
  2.5 1.2 %copy-start.1 = (bf16[1,128,4096]{2,1,0:T(8,128)(2,1)S(1)}, bf16[1,128,4096]{2,1,0:T(8,128)(2,1)}, u32[]{:S(2)}) copy-start(bf16[1,128,4096]{2,1,0:T(8,128)(2,1)} %o_hbm.1) | copy-start | bytes 3145732
  3.8 1.2 %copy-start.2 = (bf16[1,128,4096]{2,1,0:T(8,128)(2,1)S(1)}, bf16[1,128,4096]{2,1,0:T(8,128)(2,1)}, u32[]{:S(2)}) copy-start(bf16[1,128,4096]{2,1,0:T(8,128)(2,1)} %do_hbm.1) | copy-start | bytes 3145732
  5.0 0.9 %copy-start.3 = (bf16[1,128,512]{2,1,0:T(8,128)(2,1)S(1)}, bf16[1,128,512]{2,1,0:T(8,128)(2,1)}, u32[]{:S(2)}) copy-start(bf16[1,128,512]{2,1,0:T(8,128)(2,1)} %k_hbm.1) | copy-start | bytes 393220
  5.9 0.9 %copy-start.4 = (bf16[1,128,512]{2,1,0:T(8,128)(2,1)S(1)}, bf16[1,128,512]{2,1,0:T(8,128)(2,1)}, u32[]{:S(2)}) copy-start(bf16[1,128,512]{2,1,0:T(8,128)(2,1)} %v_hbm.1) | copy-start | bytes 393220
  6.8 0.8 %copy-start.7 = (f32[64,128]{1,0:T(8,128)S(1)}, f32[64,128]{1,0:T(8,128)}, u32[]{:S(2)}) copy-start(f32[64,128]{1,0:T(8,128)} %constant.2.clone.freq_ref) | copy-start | bytes 98308

commit v2 on v1

--- a/solution.py
+++ b/solution.py
@@ -22,6 +22,7 @@
 NEG_LARGE = -1.0e30
 SCALE = HD**-0.5
 LONG = 0
+N_LONG = 3
 MESH = pl.DeviceIdType.MESH
 F32 = jnp.float32
 BF16 = jnp.bfloat16
@@ -65,9 +66,9 @@
 
 def kernel(
     n_ctx,
-    doc_ref, fetch_ref, freq_ref, q_hbm, k_hbm, v_hbm, o_hbm, do_hbm,
+    doc_hbm, fetch_hbm, freq_hbm, q_hbm, k_hbm, v_hbm, o_hbm, do_hbm,
     out_ref, dk_ref, dv_ref,
-    q_in, k_in, o_in, do_in,
+    doc_ref, fetch_ref, freq_ref, q_in, k_in, o_in, do_in,
     kv, qr, doz, bias, tab_t, tab_c, tab_s, k_t, p_win, ds_win, own, back_out, back_in, dq, relay,
     in_sem, kv_send, kv_recv, back_send, back_recv, dq_send, out_recv, relay_recv, relay_send,
 ):
@@ -80,7 +81,12 @@
     loads.append(pltpu.make_async_copy(q_hbm.at[0], q_in, in_sem.at[5]))
     loads.append(pltpu.make_async_copy(do_hbm.at[0], do_in, in_sem.at[6]))
     loads.append(pltpu.make_async_copy(o_hbm.at[0], o_in, in_sem.at[7]))
-    for load in loads:
+    small = [
+        pltpu.make_async_copy(doc_hbm, doc_ref, in_sem.at[8]),
+        pltpu.make_async_copy(freq_hbm, freq_ref, in_sem.at[9]),
+        pltpu.make_async_copy(fetch_hbm, fetch_ref, in_sem.at[10]),
+    ]
+    for load in small + loads:
         load.start()
 
     barrier = pltpu.get_barrier_semaphore()
@@ -96,6 +102,8 @@
 
     first = c * TOK
     lane_t = lax.broadcasted_iota(jnp.int32, (1, TOK), 1) + first
+    for load in small:
+        load.wait()
     start = doc_ref[...]
     factor = 0.1 * math.log(YARN_FACTOR) + 1.0
     sin, cos = sin_cos((lane_t - start).astype(F32) * freq_ref[...])
@@ -264,7 +272,8 @@
             @pl.when(s >= 1)
             def _():
                 if j == LONG:
-                    long_copy(g).start()
+                    pl.when(g < N_LONG)(long_copy(g).start)
+                    pl.when(g >= N_LONG)(direct_copy(p).start)
                 else:
                     direct_copy(p).start()
 
@@ -277,14 +286,13 @@
             back_out[d - 1, g, 1] = dv[d * TOK : (d + 1) * TOK].astype(BF16)
             pl.when(c >= d)(back_copy(g, d).start)
 
-        @pl.when(g >= 1)
+        @pl.when((g >= 1) & (g <= N_LONG))
         def _():
             forward(g - 1)
 
         return carry
 
     lax.fori_loop(0, HK, group, 0)
-    forward(HK - 1)
 
     def finish(g, carry):
         for d in (1, 2):
@@ -309,12 +317,12 @@
             for j in range(PAIRS):
                 direct_copy(g * PAIRS + j).wait_send()
 
-        @pl.when(s == 0)
+        @pl.when((s == 0) & (g < N_LONG))
         def _():
             relay_copy(0, g, 1).wait_send()
             relay_copy(1, g, 2).wait_send()
 
-        @pl.when(s == 2)
+        @pl.when((s == 2) & (g < N_LONG))
         def _():
             relay_copy(0, g, 0).wait_send()
 
@@ -331,6 +339,20 @@
         return carry
 
     lax.fori_loop(0, HK, drain, 0)
+
+
+def hand_out(a, b, c, a_out, b_out, c_out, sem):
+    copies = [
+        pltpu.make_async_copy(b, b_out, sem.at[0]),
+        pltpu.make_async_copy(c, c_out, sem.at[1]),
+    ]
+    for i in range(8):
+        rows = pl.ds(i * (TOK // 8), TOK // 8)
+        copies.append(pltpu.make_async_copy(a.at[0, rows], a_out.at[0, rows], sem.at[2 + i]))
+    for copy in copies:
+        copy.start()
+    for copy in copies:
+        copy.wait()
 
 
 def solution(mesh):
@@ -339,18 +361,22 @@
 
     def shards(q, k, v, o, do, doc_start, fetch_list):
         any_spec = pl.BlockSpec(memory_space=pl.ANY)
+        hbm = pl.BlockSpec(memory_space=pltpu.HBM)
         vmem = pl.BlockSpec(memory_space=pltpu.VMEM)
         dma = pltpu.SemaphoreType.DMA
-        return pl.pallas_call(
+        results = pl.pallas_call(
             functools.partial(kernel, n_ctx),
             out_shape=(
-                jax.ShapeDtypeStruct((1, TOK, HQ * HD), BF16),
-                jax.ShapeDtypeStruct((1, TOK, HK * HD), BF16),
-                jax.ShapeDtypeStruct((1, TOK, HK * HD), BF16),
+                pltpu.VMEM((1, TOK, HQ * HD), BF16),
+                pltpu.VMEM((1, TOK, HK * HD), BF16),
+                pltpu.VMEM((1, TOK, HK * HD), BF16),
             ),
-            in_specs=[vmem] * 3 + [any_spec] * 5,
-            out_specs=(any_spec, vmem, vmem),
+            in_specs=[hbm] * 8,
+            out_specs=(vmem,) * 3,
             scratch_shapes=[
+                pltpu.VMEM((1, TOK), jnp.int32),
+                pltpu.VMEM((1, 2), jnp.int32),
+                pltpu.VMEM((HALF, TOK), F32),
                 pltpu.VMEM((TOK, HQ * HD), BF16),
                 pltpu.VMEM((TOK, HK * HD), BF16),
                 pltpu.VMEM((TOK, HQ * HD), BF16),
@@ -370,7 +396,7 @@
                 pltpu.VMEM((2, HK, 2, TOK, HD), BF16),
                 pltpu.VMEM((HK * PAIRS, TOK, 2 * HD), BF16),
                 pltpu.VMEM((2, HK, TOK, 2 * HD), BF16),
-                dma((8,)),
+                dma((11,)),
                 dma((2, HK)),
                 dma((2, HK)),
                 dma((2, HK)),
@@ -381,10 +407,19 @@
                 dma((2, HK)),
             ],
             compiler_params=pltpu.CompilerParams(
-                collective_id=0, has_side_effects=True, vmem_limit_bytes=24 << 20
+                collective_id=0, has_side_effects=True, vmem_limit_bytes=28 << 20
             ),
             cost_estimate=pl.CostEstimate(flops=2_000_000_000, bytes_accessed=5_000_000, transcendentals=1_600_000),
-        )(doc_start.reshape(1, TOK), fetch_list, jnp.asarray(freq), q, k, v, o, do)
+        )(*(pltpu.with_memory_space_constraint(x, pltpu.HBM) for x in (doc_start.reshape(1, TOK), fetch_list, jnp.asarray(freq), q, k, v, o, do)))
+        return pl.pallas_call(
+            hand_out,
+            out_shape=tuple(jax.ShapeDtypeStruct((1, TOK, n * HD), BF16) for n in (HQ, HK, HK)),
+            in_specs=[vmem] * 3,
+            out_specs=(hbm,) * 3,
+            scratch_shapes=[dma((10,))],
+            compiler_params=pltpu.CompilerParams(vmem_limit_bytes=1 << 20),
+            cost_estimate=pl.CostEstimate(flops=0, bytes_accessed=2_600_000, transcendentals=0),
+        )(*results)
 
     return jax.shard_map(
         shards,

time: 45.9 us -> 34.9 us (0.76)
  local copies, waits for them, and re-layouts: 9.18 us -> 0 us
  Pallas kernels: 35.4 us -> 33.6 us
    unnamed x19 -> x0, local copies, waits for them, and re-layouts: 9.18 us -> none
    pallas_call x1 -> x2, Pallas kernels: 35.4 us -> 33.6 us  [the longest x1 32.4 us: shards(): pl.pallas_call(functools.partial(kernel, n_ctx), out_shape=(pltpu.VMEM((1...]
where the time goes in v2:
time: 34.9 us; the launch traced here: 34.2 us
  Pallas kernels  33.6 us (96%)
  between operations  0.64 us (2%)
    pallas_call x1, Pallas kernels, shards(): pl.pallas_call(functools.partial(kernel, n_ctx), out_shape=(pltpu.VMEM((1...  32.4 us
    pallas_call x1, Pallas kernels, shards(): pl.pallas_call(hand_out, out_shape=tuple((jax.ShapeDtypeStruct((1, TOK, n...  1.13 us

profile of v2, /device:TPU:20, one launch (start us, length us, event | category | flops | bytes accessed | tf_op | source)
XLA Modules:
  0.0 34.2 jit_solution(4468722115405391908)
XLA Ops:
  0.6 32.4 %shard_map.103 = (bf16[1,128,4096]{2,1,0:T(8,128)(2,1)S(1)}, bf16[1,128,512]{2,1,0:T(8,128)(2,1)S(1)}, bf16[1,128,512]{2,1,0:T(8,128)(2,1)S(1)}) custom-call(s32[1,128]{1,0:T(1,128)} %bitcast.1, s32[1,2]{1,0:T(1,128)} %fetch_hbm.1, f32[64,128]{1,0:T(8,128)} %constant.2.clone.freq_hbm, bf16[1,128,4096]{2,1,0:T(8,128)(2,1)} %q_hbm.1, ...), custom_call_target="tpu_custom_call" | custom-call | flops 2000000000 | bytes 5000000 | tf_op jit(solution)/shard_map/pallas_call | solution.py:367
  33.1 1.1 %shard_map.104 = (bf16[1,128,4096]{2,1,0:T(8,128)(2,1)}, bf16[1,128,512]{2,1,0:T(8,128)(2,1)}, bf16[1,128,512]{2,1,0:T(8,128)(2,1)}) custom-call(bf16[1,128,4096]{2,1,0:T(8,128)(2,1)S(1)} %get-tuple-element.6.a, bf16[1,128,512]{2,1,0:T(8,128)(2,1)S(1)} %get-tuple-element.7.b, bf16[1,128,512]{2,1,0:T(8,128)(2,1)S(1)} %get-tuple-element.8.c), custom_call_target="tpu_custom_call" | custom-call | bytes 2600000 | tf_op jit(solution)/shard_map/pallas_call | solution.py:414

commit v3 on v2

--- a/solution.py
+++ b/solution.py
@@ -23,6 +23,7 @@
 SCALE = HD**-0.5
 LONG = 0
 N_LONG = 3
+RELAY = 1
 MESH = pl.DeviceIdType.MESH
 F32 = jnp.float32
 BF16 = jnp.bfloat16
@@ -68,86 +69,111 @@
     n_ctx,
     doc_hbm, fetch_hbm, freq_hbm, q_hbm, k_hbm, v_hbm, o_hbm, do_hbm,
     out_ref, dk_ref, dv_ref,
-    doc_ref, fetch_ref, freq_ref, q_in, k_in, o_in, do_in,
+    doc_ref, fetch_ref, freq_ref, q_in, o_in, do_in,
     kv, qr, doz, bias, tab_t, tab_c, tab_s, k_t, p_win, ds_win, own, back_out, back_in, dq, relay,
-    in_sem, kv_send, kv_recv, back_send, back_recv, dq_send, out_recv, relay_recv, relay_send,
+    ready, small_sem, kv_sem, query_sem, kv_send, kv_recv, back_send, back_recv, dq_send, out_recv, relay_recv, relay_send,
 ):
     c = lax.axis_index("ctx")
     s = lax.axis_index("section")
 
-    loads = [pltpu.make_async_copy(k_hbm.at[0], k_in, in_sem.at[0])]
+    small = [
+        pltpu.make_async_copy(doc_hbm, doc_ref, small_sem.at[0]),
+        pltpu.make_async_copy(freq_hbm, freq_ref, small_sem.at[1]),
+        pltpu.make_async_copy(fetch_hbm, fetch_ref, small_sem.at[2]),
+    ]
+
+    def head_cols(ref, g):
+        return ref.at[0, :, pl.ds(pl.multiple_of(g * HD, HD), HD)]
+
+    def kv_loads(g):
+        return [
+            pltpu.make_async_copy(head_cols(x, g), kv.at[0, g, i], kv_sem.at[i, g]) for i, x in enumerate((k_hbm, v_hbm))
+        ]
+
+    def query_loads(g):
+        cols = pl.ds(pl.multiple_of(g * RATIO * HD, RATIO * HD), RATIO * HD)
+        return [
+            pltpu.make_async_copy(x.at[0, :, cols], y.at[g], query_sem.at[i, g])
+            for i, (x, y) in enumerate(((q_hbm, q_in), (do_hbm, do_in), (o_hbm, o_in)))
+        ]
+
+    for load in small:
+        load.start()
     for g in range(HK):
-        loads.append(pltpu.make_async_copy(v_hbm.at[0, :, pl.ds(g * HD, HD)], kv.at[0, g, 1], in_sem.at[1 + g]))
-    loads.append(pltpu.make_async_copy(q_hbm.at[0], q_in, in_sem.at[5]))
-    loads.append(pltpu.make_async_copy(do_hbm.at[0], do_in, in_sem.at[6]))
-    loads.append(pltpu.make_async_copy(o_hbm.at[0], o_in, in_sem.at[7]))
-    small = [
-        pltpu.make_async_copy(doc_hbm, doc_ref, in_sem.at[8]),
-        pltpu.make_async_copy(freq_hbm, freq_ref, in_sem.at[9]),
-        pltpu.make_async_copy(fetch_hbm, fetch_ref, in_sem.at[10]),
-    ]
-    for load in small + loads:
-        load.start()
+        for load in kv_loads(g) + query_loads(g):
+            load.start()
 
     barrier = pltpu.get_barrier_semaphore()
     for d in (1, 2):
         @pl.when(c >= d)
         def _():
             pl.semaphore_signal(barrier, inc=1, device_id=(c - d, s), device_id_type=MESH)
-    for me, others in ((0, (1, 2, 3)), (1, (0, 2)), (2, (0, 1, 3))):
+    for me, others in ((0, (1, 2, 3)), (1, (2,)), (2, (3,))):
         @pl.when(s == me)
         def _():
             for other in others:
                 pl.semaphore_signal(barrier, inc=1, device_id=(c, other), device_id_type=MESH)
 
-    first = c * TOK
-    lane_t = lax.broadcasted_iota(jnp.int32, (1, TOK), 1) + first
+    greeted = s - s // 3 + (c < n_ctx - 1).astype(jnp.int32) + (c < n_ctx - 2).astype(jnp.int32)
+
+    @pl.when(greeted > 0)
+    def _():
+        pl.semaphore_wait(barrier, greeted)
+
+    for me, others in ((1, (0,)), (2, (0, 1))):
+        @pl.when(s == me)
+        def _():
+            for other in others:
+                pl.semaphore_signal(ready, inc=1, device_id=(c, other), device_id_type=MESH)
+
+    def kv_copies(g, d):
+        return [
+            pltpu.make_async_remote_copy(
+                src_ref=head_cols(x, g), dst_ref=kv.at[d, g, i],
+                send_sem=kv_send.at[d - 1, g, i], recv_sem=kv_recv.at[d - 1, g, i],
+                device_id=(c + d, s), device_id_type=MESH,
+            )
+            for i, x in enumerate((k_hbm, v_hbm))
+        ]
+
+    for g in range(1):
+        for d in (1, 2):
+            @pl.when(c < n_ctx - d)
+            def _():
+                for copy in kv_copies(g, d):
+                    copy.start()
+    for d in (1, 2):
+        @pl.when(c < d)
+        def _():
+            kv[d] = jnp.zeros((HK, 2, TOK, HD), BF16)
+        @pl.when(c >= n_ctx - d)
+        def _():
+            back_in[d - 1] = jnp.zeros((HK, 2, TOK, HD), BF16)
+
     for load in small:
         load.wait()
+    first = c * TOK
+    lane = lax.broadcasted_iota(jnp.int32, (1, TOK), 1)
+    lane_t = lane + first
     start = doc_ref[...]
     factor = 0.1 * math.log(YARN_FACTOR) + 1.0
-    sin, cos = sin_cos((lane_t - start).astype(F32) * freq_ref[...])
-    sin = sin * factor
-    cos = cos * factor
-    tab_t[0] = cos * SCALE
-    tab_t[1] = sin * SCALE
-    turned = jnp.concatenate([cos, sin], axis=0).T
-    swapped = pltpu.roll(turned, HALF, 1)
     low = lax.broadcasted_iota(jnp.int32, (TOK, HD), 1) < HALF
-    tab_c[...] = jnp.where(low, turned, swapped)
-    tab_s[...] = jnp.where(low, -swapped, turned)
-
-    def rope(x):
+    for d in range(3):
+        position = lane_t - start if d == 0 else jnp.maximum(lane_t - d * TOK - start[:, 0:1], 0)
+        sin, cos = sin_cos(position.astype(F32) * freq_ref[...])
+        sin = sin * factor
+        cos = cos * factor
+        if d == 0:
+            tab_t[0] = cos * SCALE
+            tab_t[1] = sin * SCALE
+        turned = jnp.concatenate([cos, sin], axis=0).T
+        swapped = pltpu.roll(turned, HALF, 1)
+        tab_c[d] = jnp.where(low, turned, swapped)
+        tab_s[d] = jnp.where(low, -swapped, turned)
+
+    def rope(x, d):
         x = x.astype(F32)
-        return (x * tab_c[...] + pltpu.roll(x, HALF, 1) * tab_s[...]).astype(BF16)
-
-    loads[0].wait()
-    for g in range(HK):
-        kv[0, g, 0] = rope(k_in[:, g * HD : (g + 1) * HD])
-    for g in range(HK):
-        loads[1 + g].wait()
-
-    pl.semaphore_wait(
-        barrier, 2 + (c < n_ctx - 1).astype(jnp.int32) + (c < n_ctx - 2).astype(jnp.int32)
-    )
-
-    def kv_copy(g, d):
-        return pltpu.make_async_remote_copy(
-            src_ref=kv.at[0, g], dst_ref=kv.at[d, g],
-            send_sem=kv_send.at[d - 1, g], recv_sem=kv_recv.at[d - 1, g],
-            device_id=(c + d, s), device_id_type=MESH,
-        )
-
-    for g in range(HK):
-        for d in (1, 2):
-            pl.when(c < n_ctx - d)(kv_copy(g, d).start)
-    for d in (1, 2):
-        @pl.when(c < d)
-        def _():
-            kv[d] = jnp.zeros((HK, 2, TOK, HD), BF16)
-        @pl.when(c >= n_ctx - d)
-        def _():
-            back_in[d - 1] = jnp.zeros((HK, 2, TOK, HD), BF16)
+        return (x * tab_c[d] + pltpu.roll(x, HALF, 1) * tab_s[d]).astype(BF16)
 
     def zero_copy(p):
         return pltpu.make_async_copy(
@@ -172,22 +198,30 @@
             allowed = allowed & (fetch_ref[:, d - 1 : d] == 1)
         bias[d * TOK : (d + 1) * TOK, :] = jnp.where(allowed, 0.0, NEG_LARGE)
 
-    loads[5].wait()
-    loads[6].wait()
-    loads[7].wait()
-
-    def prepare(h, carry):
-        cols = pl.ds(pl.multiple_of(h * HD, HD), HD)
-        qr[h] = rope(q_in[:, cols])
-        grad = do_in[:, cols]
-        prod = grad.astype(F32) * o_in[:, cols].astype(F32)
-        prod = prod + pltpu.roll(prod, HALF, 1)
-        high = prod.astype(BF16).astype(F32)
-        doz[h, :, 0:HD] = grad
-        doz[h, :, HD : 2 * HD] = jnp.where(low, high, prod - high).astype(BF16)
-        return carry
-
-    lax.fori_loop(0, HQ, prepare, 0)
+    for g in range(HK):
+        for load in query_loads(g) + kv_loads(g):
+            load.wait()
+
+    def prepare(g):
+        for i in range(RATIO):
+            h = g * RATIO + i
+            cols = slice(i * HD, (i + 1) * HD)
+            qr[h] = rope(q_in[g, :, cols], 0)
+            grad = do_in[g, :, cols]
+            prod = grad.astype(F32) * o_in[g, :, cols].astype(F32)
+            prod = prod + pltpu.roll(prod, HALF, 1)
+            high = prod.astype(BF16).astype(F32)
+            doz[h, :, 0:HD] = grad
+            doz[h, :, HD : 2 * HD] = jnp.where(low, high, prod - high).astype(BF16)
+
+    lax.fori_loop(0, HK, lambda g, c: (prepare(g), c)[1], 0)
+
+    for g in range(1, HK):
+        for d in (1, 2):
+            @pl.when(c < n_ctx - d)
+            def _():
+                for copy in kv_copies(g, d):
+                    copy.start()
 
     def out_cols(p):
         return out_ref.at[0, :, pl.ds(pl.multiple_of(p * 2 * HD, 2 * HD), 2 * HD)]
@@ -223,6 +257,10 @@
     def forward(g):
         @pl.when(s == 0)
         def _():
+            @pl.when(g == 0)
+            def _():
+                pl.semaphore_wait(ready, 2)
+
             arrival(0, g).wait_recv()
             relay_copy(0, g, 1).start()
             arrival(1, g).wait_recv()
@@ -242,8 +280,12 @@
 
     def group(g, carry):
         for d in (1, 2):
-            pl.when(c >= d)(kv_copy(g, d).wait_recv)
-        k_win = jnp.concatenate([kv[d, g, 0] for d in range(3)], axis=0)
+            @pl.when(c >= d)
+            def _():
+                for copy in kv_copies(g, d):
+                    copy.wait_recv()
+
+        k_win = jnp.concatenate([rope(kv[d, g, 0], d) for d in range(3)], axis=0)
         v_win = jnp.concatenate([kv[d, g, 1] for d in range(3)], axis=0)
         v_one = jnp.concatenate([v_win, jnp.full((3 * TOK, HD), -1.0, BF16)], axis=1)
         k_t[...] = k_win.T
@@ -269,6 +311,11 @@
                 )
                 dq[p, :, i * HD : (i + 1) * HD] = grad.T.astype(BF16)
 
+            if j == LONG:
+                @pl.when((s == 1) & (g == 0))
+                def _():
+                    pl.semaphore_wait(ready, 1)
+
             @pl.when(s >= 1)
             def _():
                 if j == LONG:
@@ -301,7 +348,7 @@
         dv = own[g, 1] + back_in[0, g, 1].astype(F32) + back_in[1, g, 1].astype(F32)
         dk = dk * SCALE
         cols = pl.ds(pl.multiple_of(g * HD, HD), HD)
-        dk_ref[0, :, cols] = (dk * tab_c[...] - pltpu.roll(dk, HALF, 1) * tab_s[...]).astype(BF16)
+        dk_ref[0, :, cols] = (dk * tab_c[0] - pltpu.roll(dk, HALF, 1) * tab_s[0]).astype(BF16)
         dv_ref[0, :, cols] = dv.astype(BF16)
         return carry
 
@@ -309,7 +356,11 @@
 
     def drain(g, carry):
         for d in (1, 2):
-            pl.when(c < n_ctx - d)(kv_copy(g, d).wait_send)
+            @pl.when(c < n_ctx - d)
+            def _():
+                for copy in kv_copies(g, d):
+                    copy.wait_send()
+
             pl.when(c >= d)(back_copy(g, d).wait_send)
 
         @pl.when(s >= 1)
@@ -377,17 +428,16 @@
                 pltpu.VMEM((1, TOK), jnp.int32),
                 pltpu.VMEM((1, 2), jnp.int32),
                 pltpu.VMEM((HALF, TOK), F32),
-                pltpu.VMEM((TOK, HQ * HD), BF16),
-                pltpu.VMEM((TOK, HK * HD), BF16),
-                pltpu.VMEM((TOK, HQ * HD), BF16),
-                pltpu.VMEM((TOK, HQ * HD), BF16),
+                pltpu.VMEM((HK, TOK, RATIO * HD), BF16),
+                pltpu.VMEM((HK, TOK, RATIO * HD), BF16),
+                pltpu.VMEM((HK, TOK, RATIO * HD), BF16),
                 pltpu.VMEM((3, HK, 2, TOK, HD), BF16),
                 pltpu.VMEM((HQ, TOK, HD), BF16),
                 pltpu.VMEM((HQ, TOK, 2 * HD), BF16),
                 pltpu.VMEM((3 * TOK, TOK), F32),
                 pltpu.VMEM((2, HALF, TOK), F32),
-                pltpu.VMEM((TOK, HD), F32),
-                pltpu.VMEM((TOK, HD), F32),
+                pltpu.VMEM((3, TOK, HD), F32),
+                pltpu.VMEM((3, TOK, HD), F32),
                 pltpu.VMEM((HD, 3 * TOK), BF16),
                 pltpu.VMEM((3 * TOK, RATIO * TOK), BF16),
                 pltpu.VMEM((3 * TOK, RATIO * TOK), BF16),
@@ -396,9 +446,12 @@
                 pltpu.VMEM((2, HK, 2, TOK, HD), BF16),
                 pltpu.VMEM((HK * PAIRS, TOK, 2 * HD), BF16),
                 pltpu.VMEM((2, HK, TOK, 2 * HD), BF16),
-                dma((11,)),
+                pltpu.SemaphoreType.REGULAR,
+                dma((3,)),
                 dma((2, HK)),
-                dma((2, HK)),
+                dma((3, HK)),
+                dma((2, HK, 2)),
+                dma((2, HK, 2)),
                 dma((2, HK)),
                 dma((2, HK)),
                 dma((HK * PAIRS,)),

time: 34.9 us -> 34.2 us (0.980)
  Pallas kernels: 33.6 us -> 33.2 us
    pallas_call x1, Pallas kernels: 32.4 us -> 32.1 us  [shards(): pl.pallas_call(functools.partial(kernel, n_ctx), out_shape=(pltpu.VMEM((1...]
where the time goes in v3:
time: 34.2 us; the launch traced here: 33.9 us
  Pallas kernels  33.2 us (97%)
  between operations  0.64 us (2%)
    pallas_call x1, Pallas kernels, shards(): pl.pallas_call(functools.partial(kernel, n_ctx), out_shape=(pltpu.VMEM((1...  32.1 us
    pallas_call x1, Pallas kernels, shards(): pl.pallas_call(hand_out, out_shape=tuple((jax.ShapeDtypeStruct((1, TOK, n...  1.13 us

profile of v3, /device:TPU:20, one launch (start us, length us, event | category | flops | bytes accessed | tf_op | source)
XLA Modules:
  0.0 33.9 jit_solution(10675813959463732261)
XLA Ops:
  0.6 32.1 %shard_map.103 = (bf16[1,128,4096]{2,1,0:T(8,128)(2,1)S(1)}, bf16[1,128,512]{2,1,0:T(8,128)(2,1)S(1)}, bf16[1,128,512]{2,1,0:T(8,128)(2,1)S(1)}) custom-call(s32[1,128]{1,0:T(1,128)} %bitcast.1, s32[1,2]{1,0:T(1,128)} %fetch_hbm.1, f32[64,128]{1,0:T(8,128)} %constant.2.clone.freq_hbm, bf16[1,128,4096]{2,1,0:T(8,128)(2,1)} %q_hbm.1, ...), custom_call_target="tpu_custom_call" | custom-call | flops 2000000000 | bytes 5000000 | tf_op jit(solution)/shard_map/pallas_call | solution.py:418
  32.7 1.1 %shard_map.104 = (bf16[1,128,4096]{2,1,0:T(8,128)(2,1)}, bf16[1,128,512]{2,1,0:T(8,128)(2,1)}, bf16[1,128,512]{2,1,0:T(8,128)(2,1)}) custom-call(bf16[1,128,4096]{2,1,0:T(8,128)(2,1)S(1)} %get-tuple-element.6.a, bf16[1,128,512]{2,1,0:T(8,128)(2,1)S(1)} %get-tuple-element.7.b, bf16[1,128,512]{2,1,0:T(8,128)(2,1)S(1)} %get-tuple-element.8.c), custom_call_target="tpu_custom_call" | custom-call | bytes 2600000 | tf_op jit(solution)/shard_map/pallas_call | solution.py:467

commit v4 on v3

--- a/solution.py
+++ b/solution.py
@@ -21,8 +21,10 @@
 YARN_FACTOR = 4.0
 NEG_LARGE = -1.0e30
 SCALE = HD**-0.5
-LONG = 0
+LONG = 1
 N_LONG = 3
+CHAIN = 16
+SIDE = (6, 10)
 RELAY = 1
 MESH = pl.DeviceIdType.MESH
 F32 = jnp.float32
@@ -70,11 +72,15 @@
     doc_hbm, fetch_hbm, freq_hbm, q_hbm, k_hbm, v_hbm, o_hbm, do_hbm,
     out_ref, dk_ref, dv_ref,
     doc_ref, fetch_ref, freq_ref, q_in, o_in, do_in,
-    kv, qr, doz, bias, tab_t, tab_c, tab_s, k_t, p_win, ds_win, own, back_out, back_in, dq, relay,
-    ready, small_sem, kv_sem, query_sem, kv_send, kv_recv, back_send, back_recv, dq_send, out_recv, relay_recv, relay_send,
+    kv, qr, doz, bias, tab_t, tab_c, tab_s, k_t, p_win, ds_win, own, back_out, back_in, dq, relay, side,
+    ready, helped, small_sem, kv_sem, query_sem, kv_send, kv_recv, back_send, back_recv, dq_send, out_recv, relay_recv, relay_send, side_recv, side_send,
 ):
     c = lax.axis_index("ctx")
     s = lax.axis_index("section")
+
+    place = lax.rem(c, CHAIN)
+    first_chip = (place < 2) & (s >= 1)
+    helps = [(place // 2 == i + 1) & (s <= 2) for i in range(len(SIDE))]
 
     small = [
         pltpu.make_async_copy(doc_hbm, doc_ref, small_sem.at[0]),
@@ -114,7 +120,12 @@
             for other in others:
                 pl.semaphore_signal(barrier, inc=1, device_id=(c, other), device_id_type=MESH)
 
-    greeted = s - s // 3 + (c < n_ctx - 1).astype(jnp.int32) + (c < n_ctx - 2).astype(jnp.int32)
+    @pl.when(first_chip)
+    def _():
+        for i in range(len(SIDE)):
+            pl.semaphore_signal(barrier, inc=1, device_id=(c + 2 * i + 2, s - 1), device_id_type=MESH)
+
+    greeted = s - s // 3 + sum(h.astype(jnp.int32) for h in helps) + (c < n_ctx - 1).astype(jnp.int32) + (c < n_ctx - 2).astype(jnp.int32)
 
     @pl.when(greeted > 0)
     def _():
@@ -125,6 +136,11 @@
         def _():
             for other in others:
                 pl.semaphore_signal(ready, inc=1, device_id=(c, other), device_id_type=MESH)
+
+    for i in range(len(SIDE)):
+        @pl.when(helps[i])
+        def _():
+            pl.semaphore_signal(helped, inc=1, device_id=(c - 2 * i - 2, s + 1), device_id_type=MESH)
 
     def kv_copies(g, d):
         return [
@@ -239,6 +255,20 @@
             device_id=(c, 2 * (1 - s // 2)), device_id_type=MESH,
         )
 
+    def side_copy(i):
+        return pltpu.make_async_remote_copy(
+            src_ref=dq.at[SIDE[i]], dst_ref=side.at[i],
+            send_sem=dq_send.at[SIDE[i]], recv_sem=side_recv.at[i],
+            device_id=(c + 2 * i + 2, s - 1), device_id_type=MESH,
+        )
+
+    def side_back(i):
+        return pltpu.make_async_remote_copy(
+            src_ref=side.at[i], dst_ref=out_cols(SIDE[i]),
+            send_sem=side_send.at[i], recv_sem=out_recv.at[SIDE[i]],
+            device_id=(c - 2 * i - 2, s), device_id_type=MESH,
+        )
+
     def relay_copy(slot, g, target):
         p = g * PAIRS + LONG
         return pltpu.make_async_remote_copy(
@@ -302,14 +332,10 @@
             ds = (prob * dot_t(v_one, dp_in)).astype(BF16)
             p_win[:, 2 * j * TOK : 2 * (j + 1) * TOK] = prob.astype(BF16)
             ds_win[:, 2 * j * TOK : 2 * (j + 1) * TOK] = ds
-            turned_grad = dot(k_t[...], ds)
-            for i in range(2):
-                x = turned_grad[:HALF, i * TOK : (i + 1) * TOK]
-                y = turned_grad[HALF:, i * TOK : (i + 1) * TOK]
-                grad = jnp.concatenate(
-                    [x * tab_t[0] + y * tab_t[1], y * tab_t[0] - x * tab_t[1]], axis=0
-                )
-                dq[p, :, i * HD : (i + 1) * HD] = grad.T.astype(BF16)
+            if j == 0:
+                @pl.when(first_chip & (g == 1))
+                def _():
+                    pl.semaphore_wait(helped, len(SIDE))
 
             if j == LONG:
                 @pl.when((s == 1) & (g == 0))
@@ -318,9 +344,24 @@
 
             @pl.when(s >= 1)
             def _():
+                turned_grad = dot(k_t[...], ds_win[:, 2 * j * TOK : 2 * (j + 1) * TOK])
+                for i in range(2):
+                    x = turned_grad[:HALF, i * TOK : (i + 1) * TOK]
+                    y = turned_grad[HALF:, i * TOK : (i + 1) * TOK]
+                    grad = jnp.concatenate(
+                        [x * tab_t[0] + y * tab_t[1], y * tab_t[0] - x * tab_t[1]], axis=0
+                    )
+                    dq[p, :, i * HD : (i + 1) * HD] = grad.T.astype(BF16)
                 if j == LONG:
                     pl.when(g < N_LONG)(long_copy(g).start)
                     pl.when(g >= N_LONG)(direct_copy(p).start)
+                elif j == 2:
+                    aside = first_chip & ((g == 1) | (g == 2))
+                    for i in range(len(SIDE)):
+                        pl.when(first_chip & (p == SIDE[i]))(side_copy(i).start)
+                    pl.when((g < 3) & jnp.logical_not(aside))(direct_copy(p).start)
+                elif j == 3:
+                    pl.when(g < 2)(direct_copy(p).start)
                 else:
                     direct_copy(p).start()
 
@@ -333,13 +374,30 @@
             back_out[d - 1, g, 1] = dv[d * TOK : (d + 1) * TOK].astype(BF16)
             pl.when(c >= d)(back_copy(g, d).start)
 
-        @pl.when((g >= 1) & (g <= N_LONG))
+        @pl.when((g >= 1) & (g <= N_LONG) & (s == 2))
         def _():
             forward(g - 1)
 
         return carry
 
     lax.fori_loop(0, HK, group, 0)
+
+    @pl.when(s == 0)
+    def _():
+        for g in range(N_LONG):
+            forward(g)
+
+    @pl.when(s >= 1)
+    def _():
+        for p in (11, 14, 15):
+            direct_copy(p).start()
+
+    for i in range(len(SIDE)):
+        @pl.when(helps[i])
+        def _():
+            side_copy(i).wait_recv()
+            side_back(i).start()
+
 
     def finish(g, carry):
         for d in (1, 2):
@@ -390,6 +448,9 @@
         return carry
 
     lax.fori_loop(0, HK, drain, 0)
+
+    for i in range(len(SIDE)):
+        pl.when(helps[i])(side_back(i).wait_send)
 
 
 def hand_out(a, b, c, a_out, b_out, c_out, sem):
@@ -446,6 +507,8 @@
                 pltpu.VMEM((2, HK, 2, TOK, HD), BF16),
                 pltpu.VMEM((HK * PAIRS, TOK, 2 * HD), BF16),
                 pltpu.VMEM((2, HK, TOK, 2 * HD), BF16),
+                pltpu.VMEM((len(SIDE), TOK, 2 * HD), BF16),
+                pltpu.SemaphoreType.REGULAR,
                 pltpu.SemaphoreType.REGULAR,
                 dma((3,)),
                 dma((2, HK)),
@@ -458,6 +521,8 @@
                 dma((HK * PAIRS,)),
                 dma((2, HK)),
                 dma((2, HK)),
+                dma((len(SIDE),)),
+                dma((len(SIDE),)),
             ],
             compiler_params=pltpu.CompilerParams(
                 collective_id=0, has_side_effects=True, vmem_limit_bytes=28 << 20

time: 34.2 us -> 33.2 us (0.971)
  Pallas kernels: 33.2 us -> 32.2 us
    pallas_call x1, Pallas kernels: 32.1 us -> 31 us  [shards(): pl.pallas_call(functools.partial(kernel, n_ctx), out_shape=(pltpu.VMEM((1...]
where the time goes in v4:
time: 33.2 us; the launch traced here: 32.8 us
  Pallas kernels  32.2 us (97%)
  between operations  0.64 us (2%)
    pallas_call x1, Pallas kernels, shards(): pl.pallas_call(functools.partial(kernel, n_ctx), out_shape=(pltpu.VMEM((1...  31 us
    pallas_call x1, Pallas kernels, shards(): pl.pallas_call(hand_out, out_shape=tuple((jax.ShapeDtypeStruct((1, TOK, n...  1.13 us

profile of v4, /device:TPU:20, one launch (start us, length us, event | category | flops | bytes accessed | tf_op | source)
XLA Modules:
  0.0 32.8 jit_solution(7350378986897905180)
XLA Ops:
  0.6 31.0 %shard_map.103 = (bf16[1,128,4096]{2,1,0:T(8,128)(2,1)S(1)}, bf16[1,128,512]{2,1,0:T(8,128)(2,1)S(1)}, bf16[1,128,512]{2,1,0:T(8,128)(2,1)S(1)}) custom-call(s32[1,128]{1,0:T(1,128)} %bitcast.1, s32[1,2]{1,0:T(1,128)} %fetch_hbm.1, f32[64,128]{1,0:T(8,128)} %constant.2.clone.freq_hbm, bf16[1,128,4096]{2,1,0:T(8,128)(2,1)} %q_hbm.1, ...), custom_call_target="tpu_custom_call" | custom-call | flops 2000000000 | bytes 5000000 | tf_op jit(solution)/shard_map/pallas_call | solution.py:479
  31.7 1.1 %shard_map.104 = (bf16[1,128,4096]{2,1,0:T(8,128)(2,1)}, bf16[1,128,512]{2,1,0:T(8,128)(2,1)}, bf16[1,128,512]{2,1,0:T(8,128)(2,1)}) custom-call(bf16[1,128,4096]{2,1,0:T(8,128)(2,1)S(1)} %get-tuple-element.6.a, bf16[1,128,512]{2,1,0:T(8,128)(2,1)S(1)} %get-tuple-element.7.b, bf16[1,128,512]{2,1,0:T(8,128)(2,1)S(1)} %get-tuple-element.8.c), custom_call_target="tpu_custom_call" | custom-call | bytes 2600000 | tf_op jit(solution)/shard_map/pallas_call | solution.py:532

commit v5 on v4

--- a/solution.py
+++ b/solution.py
@@ -21,10 +21,9 @@
 YARN_FACTOR = 4.0
 NEG_LARGE = -1.0e30
 SCALE = HD**-0.5
-LONG = 1
 N_LONG = 3
 CHAIN = 16
-SIDE = (6, 10)
+SIDE = (7, 10)
 RELAY = 1
 MESH = pl.DeviceIdType.MESH
 F32 = jnp.float32
@@ -57,6 +56,10 @@
     s = jnp.where(odd, cos, sin)
     c = jnp.where(odd, sin, cos)
     return jnp.where(q >= 2, -s, s), jnp.where((q == 1) | (q == 2), -c, c)
+
+
+def long_pair(i, early):
+    return i * PAIRS + 1 - jnp.minimum(i, 1) - 2 * early * (i // 2)
 
 
 def dot_t(a, b):
@@ -250,8 +253,8 @@
 
     def long_copy(g):
         return pltpu.make_async_remote_copy(
-            src_ref=dq.at[g * PAIRS + LONG], dst_ref=relay.at[s // 3, g],
-            send_sem=dq_send.at[g * PAIRS + LONG], recv_sem=relay_recv.at[s // 3, g],
+            src_ref=dq.at[long_pair(g, s // 3)], dst_ref=relay.at[s // 3, g],
+            send_sem=dq_send.at[long_pair(g, s // 3)], recv_sem=relay_recv.at[s // 3, g],
             device_id=(c, 2 * (1 - s // 2)), device_id_type=MESH,
         )
 
@@ -270,7 +273,7 @@
         )
 
     def relay_copy(slot, g, target):
-        p = g * PAIRS + LONG
+        p = long_pair(g, slot)
         return pltpu.make_async_remote_copy(
             src_ref=relay.at[slot, g], dst_ref=out_cols(p),
             send_sem=relay_send.at[slot, g], recv_sem=out_recv.at[p],
@@ -279,8 +282,8 @@
 
     def arrival(slot, g):
         return pltpu.make_async_remote_copy(
-            src_ref=dq.at[g * PAIRS + LONG], dst_ref=relay.at[slot, g],
-            send_sem=dq_send.at[g * PAIRS + LONG], recv_sem=relay_recv.at[slot, g],
+            src_ref=dq.at[0], dst_ref=relay.at[slot, g],
+            send_sem=dq_send.at[0], recv_sem=relay_recv.at[slot, g],
             device_id=(c, 0), device_id_type=MESH,
         )
 
@@ -319,17 +322,25 @@
         v_win = jnp.concatenate([kv[d, g, 1] for d in range(3)], axis=0)
         v_one = jnp.concatenate([v_win, jnp.full((3 * TOK, HD), -1.0, BF16)], axis=1)
         k_t[...] = k_win.T
-        for j in range(PAIRS):
-            p = g * PAIRS + j
+        b = bias[...]
+        b = jnp.concatenate([b, b], axis=1)
+
+        def products(j):
             h = g * RATIO + 2 * j
             qp = qr[pl.ds(h, 2)].reshape(2 * TOK, HD)
             dp_in = doz[pl.ds(h, 2)].reshape(2 * TOK, 2 * HD)
-            sc = dot_t(k_win, qp) * (SCALE * math.log2(math.e))
-            b = bias[...]
-            sc = sc + jnp.concatenate([b, b], axis=1)
+            return dot_t(k_win, qp), dot_t(v_one, dp_in)
+
+        ahead = products(0)
+        for j in range(PAIRS):
+            p = g * PAIRS + j
+            sc, dp = ahead
+            if j + 1 < PAIRS:
+                ahead = products(j + 1)
+            sc = sc * (SCALE * math.log2(math.e)) + b
             e = jnp.exp2(sc - jnp.max(sc, axis=0, keepdims=True))
             prob = e * (1.0 / jnp.sum(e, axis=0, keepdims=True))
-            ds = (prob * dot_t(v_one, dp_in)).astype(BF16)
+            ds = (prob * dp).astype(BF16)
             p_win[:, 2 * j * TOK : 2 * (j + 1) * TOK] = prob.astype(BF16)
             ds_win[:, 2 * j * TOK : 2 * (j + 1) * TOK] = ds
             if j == 0:
@@ -337,7 +348,7 @@
                 def _():
                     pl.semaphore_wait(helped, len(SIDE))
 
-            if j == LONG:
+            if j == 1:
                 @pl.when((s == 1) & (g == 0))
                 def _():
                     pl.semaphore_wait(ready, 1)
@@ -352,18 +363,23 @@
                         [x * tab_t[0] + y * tab_t[1], y * tab_t[0] - x * tab_t[1]], axis=0
                     )
                     dq[p, :, i * HD : (i + 1) * HD] = grad.T.astype(BF16)
-                if j == LONG:
-                    pl.when(g < N_LONG)(long_copy(g).start)
-                    pl.when(g >= N_LONG)(direct_copy(p).start)
+                if j == 0:
+                    far = (g == 1) | ((g == 2) & (s < 3))
+                    pl.when(far)(long_copy(g).start)
+                    pl.when(jnp.logical_not(far))(direct_copy(p).start)
+                elif j == 1:
+                    pl.when(g == 0)(long_copy(g).start)
+                    pl.when(g >= 1)(direct_copy(p).start)
                 elif j == 2:
-                    aside = first_chip & ((g == 1) | (g == 2))
-                    for i in range(len(SIDE)):
-                        pl.when(first_chip & (p == SIDE[i]))(side_copy(i).start)
-                    pl.when((g < 3) & jnp.logical_not(aside))(direct_copy(p).start)
-                elif j == 3:
-                    pl.when(g < 2)(direct_copy(p).start)
+                    far = (g == 1) & (s == 3)
+                    aside = (g == 2) & first_chip
+                    pl.when(far)(long_copy(2).start)
+                    pl.when(aside)(side_copy(1).start)
+                    pl.when((g < 3) & jnp.logical_not(far | aside))(direct_copy(p).start)
                 else:
-                    direct_copy(p).start()
+                    aside = (g == 1) & first_chip
+                    pl.when(aside)(side_copy(0).start)
+                    pl.when((g < 2) & jnp.logical_not(aside))(direct_copy(p).start)
 
         dk = dot(ds_win[...], qr[pl.ds(g * RATIO, RATIO)].reshape(RATIO * TOK, HD))
         dv = dot(p_win[...], doz[pl.ds(g * RATIO, RATIO), :, 0:HD].reshape(RATIO * TOK, HD))
@@ -374,29 +390,30 @@
             back_out[d - 1, g, 1] = dv[d * TOK : (d + 1) * TOK].astype(BF16)
             pl.when(c >= d)(back_copy(g, d).start)
 
-        @pl.when((g >= 1) & (g <= N_LONG) & (s == 2))
-        def _():
-            forward(g - 1)
+        pl.when((s == 2) & (g >= 1))(lambda: forward(g - 1))
+        due = g - 2
+
+        @pl.when((s == 0) & (due >= 0))
+        def _():
+            forward(due)
 
         return carry
 
     lax.fori_loop(0, HK, group, 0)
 
-    @pl.when(s == 0)
-    def _():
-        for g in range(N_LONG):
-            forward(g)
-
-    @pl.when(s >= 1)
-    def _():
-        for p in (11, 14, 15):
-            direct_copy(p).start()
-
-    for i in range(len(SIDE)):
+    pl.when(s == 0)(lambda: forward(N_LONG - 1))
+
+
+    for i, rest in enumerate(((11,), (14, 15))):
         @pl.when(helps[i])
         def _():
             side_copy(i).wait_recv()
             side_back(i).start()
+
+        @pl.when(s >= 1)
+        def _():
+            for p in rest:
+                direct_copy(p).start()
 
 
     def finish(g, carry):

time: 33.2 us -> 32.4 us (0.976)
  Pallas kernels: 32.2 us -> 31.3 us
    pallas_call x1, Pallas kernels: 31 us -> 30.2 us  [shards(): pl.pallas_call(functools.partial(kernel, n_ctx), out_shape=(pltpu.VMEM((1...]
where the time goes in v5:
time: 32.4 us; the launch traced here: 32 us
  Pallas kernels  31.3 us (97%)
  between operations  0.64 us (2%)
    pallas_call x1, Pallas kernels, shards(): pl.pallas_call(functools.partial(kernel, n_ctx), out_shape=(pltpu.VMEM((1...  30.2 us
    pallas_call x1, Pallas kernels, shards(): pl.pallas_call(hand_out, out_shape=tuple((jax.ShapeDtypeStruct((1, TOK, n...  1.13 us

profile of v5, /device:TPU:20, one launch (start us, length us, event | category | flops | bytes accessed | tf_op | source)
XLA Modules:
  0.0 32.0 jit_solution(4532351434504655960)
XLA Ops:
  0.6 30.2 %shard_map.103 = (bf16[1,128,4096]{2,1,0:T(8,128)(2,1)S(1)}, bf16[1,128,512]{2,1,0:T(8,128)(2,1)S(1)}, bf16[1,128,512]{2,1,0:T(8,128)(2,1)S(1)}) custom-call(s32[1,128]{1,0:T(1,128)} %bitcast.1, s32[1,2]{1,0:T(1,128)} %fetch_hbm.1, f32[64,128]{1,0:T(8,128)} %constant.2.clone.freq_hbm, bf16[1,128,4096]{2,1,0:T(8,128)(2,1)} %q_hbm.1, ...), custom_call_target="tpu_custom_call" | custom-call | flops 2000000000 | bytes 5000000 | tf_op jit(solution)/shard_map/pallas_call | solution.py:496
  30.9 1.1 %shard_map.104 = (bf16[1,128,4096]{2,1,0:T(8,128)(2,1)}, bf16[1,128,512]{2,1,0:T(8,128)(2,1)}, bf16[1,128,512]{2,1,0:T(8,128)(2,1)}) custom-call(bf16[1,128,4096]{2,1,0:T(8,128)(2,1)S(1)} %get-tuple-element.6.a, bf16[1,128,512]{2,1,0:T(8,128)(2,1)S(1)} %get-tuple-element.7.b, bf16[1,128,512]{2,1,0:T(8,128)(2,1)S(1)} %get-tuple-element.8.c), custom_call_target="tpu_custom_call" | custom-call | bytes 2600000 | tf_op jit(solution)/shard_map/pallas_call | solution.py:549

commit v6 on v5

--- a/solution.py
+++ b/solution.py
@@ -375,11 +375,11 @@
                     aside = (g == 2) & first_chip
                     pl.when(far)(long_copy(2).start)
                     pl.when(aside)(side_copy(1).start)
-                    pl.when((g < 3) & jnp.logical_not(far | aside))(direct_copy(p).start)
+                    pl.when(((g < 3) | first_chip) & jnp.logical_not(far | aside))(direct_copy(p).start)
                 else:
                     aside = (g == 1) & first_chip
                     pl.when(aside)(side_copy(0).start)
-                    pl.when((g < 2) & jnp.logical_not(aside))(direct_copy(p).start)
+                    pl.when(((g < 2) | first_chip) & jnp.logical_not(aside))(direct_copy(p).start)
 
         dk = dot(ds_win[...], qr[pl.ds(g * RATIO, RATIO)].reshape(RATIO * TOK, HD))
         dv = dot(p_win[...], doz[pl.ds(g * RATIO, RATIO), :, 0:HD].reshape(RATIO * TOK, HD))
@@ -410,7 +410,7 @@
             side_copy(i).wait_recv()
             side_back(i).start()
 
-        @pl.when(s >= 1)
+        @pl.when((s >= 1) & jnp.logical_not(first_chip))
         def _():
             for p in rest:
                 direct_copy(p).start()
@@ -475,9 +475,7 @@
         pltpu.make_async_copy(b, b_out, sem.at[0]),
         pltpu.make_async_copy(c, c_out, sem.at[1]),
     ]
-    for i in range(8):
-        rows = pl.ds(i * (TOK // 8), TOK // 8)
-        copies.append(pltpu.make_async_copy(a.at[0, rows], a_out.at[0, rows], sem.at[2 + i]))
+    copies.append(pltpu.make_async_copy(a, a_out, sem.at[2]))
     for copy in copies:
         copy.start()
     for copy in copies:
@@ -551,7 +549,7 @@
             out_shape=tuple(jax.ShapeDtypeStruct((1, TOK, n * HD), BF16) for n in (HQ, HK, HK)),
             in_specs=[vmem] * 3,
             out_specs=(hbm,) * 3,
-            scratch_shapes=[dma((10,))],
+            scratch_shapes=[dma((3,))],
             compiler_params=pltpu.CompilerParams(vmem_limit_bytes=1 << 20),
             cost_estimate=pl.CostEstimate(flops=0, bytes_accessed=2_600_000, transcendentals=0),
         )(*results)

time: 32.4 us -> 32.3 us (level)
  no operation moved by 1% of the time
where the time goes in v6:
time: 32.3 us; the launch traced here: 31.9 us
  Pallas kernels  31.3 us (97%)
  between operations  0.64 us (2%)
    pallas_call x1, Pallas kernels, shards(): pl.pallas_call(functools.partial(kernel, n_ctx), out_shape=(pltpu.VMEM((1...  30.2 us
    pallas_call x1, Pallas kernels, shards(): pl.pallas_call(hand_out, out_shape=tuple((jax.ShapeDtypeStruct((1, TOK, n...  1.08 us

profile of v6, /device:TPU:20, one launch (start us, length us, event | category | flops | bytes accessed | tf_op | source)
XLA Modules:
  0.0 31.9 jit_solution(6338816278926852392)
XLA Ops:
  0.6 30.2 %shard_map.103 = (bf16[1,128,4096]{2,1,0:T(8,128)(2,1)S(1)}, bf16[1,128,512]{2,1,0:T(8,128)(2,1)S(1)}, bf16[1,128,512]{2,1,0:T(8,128)(2,1)S(1)}) custom-call(s32[1,128]{1,0:T(1,128)} %bitcast.1, s32[1,2]{1,0:T(1,128)} %fetch_hbm.1, f32[64,128]{1,0:T(8,128)} %constant.2.clone.freq_hbm, bf16[1,128,4096]{2,1,0:T(8,128)(2,1)} %q_hbm.1, ...), custom_call_target="tpu_custom_call" | custom-call | flops 2000000000 | bytes 5000000 | tf_op jit(solution)/shard_map/pallas_call | solution.py:494
  30.9 1.1 %shard_map.104 = (bf16[1,128,4096]{2,1,0:T(8,128)(2,1)}, bf16[1,128,512]{2,1,0:T(8,128)(2,1)}, bf16[1,128,512]{2,1,0:T(8,128)(2,1)}) custom-call(bf16[1,128,4096]{2,1,0:T(8,128)(2,1)S(1)} %get-tuple-element.6.a, bf16[1,128,512]{2,1,0:T(8,128)(2,1)S(1)} %get-tuple-element.7.b, bf16[1,128,512]{2,1,0:T(8,128)(2,1)S(1)} %get-tuple-element.8.c), custom_call_target="tpu_custom_call" | custom-call | bytes 2600000 | tf_op jit(solution)/shard_map/pallas_call | solution.py:547

commit v7 on v6

--- a/solution.py
+++ b/solution.py
@@ -155,12 +155,9 @@
             for i, x in enumerate((k_hbm, v_hbm))
         ]
 
-    for g in range(1):
-        for d in (1, 2):
-            @pl.when(c < n_ctx - d)
-            def _():
-                for copy in kv_copies(g, d):
-                    copy.start()
+    for i in range(2):
+        for d in (1, 2):
+            pl.when(c < n_ctx - d)(kv_copies(0, d)[i].start)
     for d in (1, 2):
         @pl.when(c < d)
         def _():
@@ -313,15 +310,14 @@
 
     def group(g, carry):
         for d in (1, 2):
-            @pl.when(c >= d)
-            def _():
-                for copy in kv_copies(g, d):
-                    copy.wait_recv()
-
+            pl.when(c >= d)(kv_copies(g, d)[0].wait_recv)
         k_win = jnp.concatenate([rope(kv[d, g, 0], d) for d in range(3)], axis=0)
+        k_t[...] = k_win.T
+        first_scores = dot_t(k_win, qr[pl.ds(g * RATIO, 2)].reshape(2 * TOK, HD))
+        for d in (1, 2):
+            pl.when(c >= d)(kv_copies(g, d)[1].wait_recv)
         v_win = jnp.concatenate([kv[d, g, 1] for d in range(3)], axis=0)
         v_one = jnp.concatenate([v_win, jnp.full((3 * TOK, HD), -1.0, BF16)], axis=1)
-        k_t[...] = k_win.T
         b = bias[...]
         b = jnp.concatenate([b, b], axis=1)
 
@@ -329,7 +325,7 @@
             h = g * RATIO + 2 * j
             qp = qr[pl.ds(h, 2)].reshape(2 * TOK, HD)
             dp_in = doz[pl.ds(h, 2)].reshape(2 * TOK, 2 * HD)
-            return dot_t(k_win, qp), dot_t(v_one, dp_in)
+            return first_scores if j == 0 else dot_t(k_win, qp), dot_t(v_one, dp_in)
 
         ahead = products(0)
         for j in range(PAIRS):

time: 32.3 us -> 31.7 us (0.981)
  Pallas kernels: 31.3 us -> 30.7 us
    pallas_call x1, Pallas kernels: 30.2 us -> 29.6 us  [shards(): pl.pallas_call(functools.partial(kernel, n_ctx), out_shape=(pltpu.VMEM((1...]
where the time goes in v7:
time: 31.7 us; the launch traced here: 31.3 us
  Pallas kernels  30.7 us (97%)
  between operations  0.64 us (2%)
    pallas_call x1, Pallas kernels, shards(): pl.pallas_call(functools.partial(kernel, n_ctx), out_shape=(pltpu.VMEM((1...  29.6 us
    pallas_call x1, Pallas kernels, shards(): pl.pallas_call(hand_out, out_shape=tuple((jax.ShapeDtypeStruct((1, TOK, n...  1.08 us

profile of v7, /device:TPU:20, one launch (start us, length us, event | category | flops | bytes accessed | tf_op | source)
XLA Modules:
  0.0 31.3 jit_solution(7563089249256176894)
XLA Ops:
  0.6 29.6 %shard_map.103 = (bf16[1,128,4096]{2,1,0:T(8,128)(2,1)S(1)}, bf16[1,128,512]{2,1,0:T(8,128)(2,1)S(1)}, bf16[1,128,512]{2,1,0:T(8,128)(2,1)S(1)}) custom-call(s32[1,128]{1,0:T(1,128)} %bitcast.1, s32[1,2]{1,0:T(1,128)} %fetch_hbm.1, f32[64,128]{1,0:T(8,128)} %constant.2.clone.freq_hbm, bf16[1,128,4096]{2,1,0:T(8,128)(2,1)} %q_hbm.1, ...), custom_call_target="tpu_custom_call" | custom-call | flops 2000000000 | bytes 5000000 | tf_op jit(solution)/shard_map/pallas_call | solution.py:490
  30.2 1.1 %shard_map.104 = (bf16[1,128,4096]{2,1,0:T(8,128)(2,1)}, bf16[1,128,512]{2,1,0:T(8,128)(2,1)}, bf16[1,128,512]{2,1,0:T(8,128)(2,1)}) custom-call(bf16[1,128,4096]{2,1,0:T(8,128)(2,1)S(1)} %get-tuple-element.6.a, bf16[1,128,512]{2,1,0:T(8,128)(2,1)S(1)} %get-tuple-element.7.b, bf16[1,128,512]{2,1,0:T(8,128)(2,1)S(1)} %get-tuple-element.8.c), custom_call_target="tpu_custom_call" | custom-call | bytes 2600000 | tf_op jit(solution)/shard_map/pallas_call | solution.py:543
